TPU v7x, 256 devices: a whole 4x4x8 slice. The times are simulated.
256 devices in a mesh: section: 64 (over z_lo, y, x, core), tp: 4 (over z_hi).
Axes of the slice: x: 4, y: 4, z: 8 (z_hi: 4, z_lo: 2; z = z_hi * 2 + z_lo), core: 2. Of those that a mesh axis runs over, the one named last changes fastest.
Arguments:
- kept_rows: bfloat16 [24576, 18432], P('section', 'tp'), may hold values from -8 to 8, as said below
- parked_rows: bfloat16 [16384, 18432], P(('section', 'tp')), may hold values from -8 to 8, as said below
- grad_out: bfloat16 [32768, 6144], P('section', 'tp'), may hold values from -6 to 6
- lengths: int32 [3], replicated, may hold values from 64 to 256, as said below
- evicted: int32 [64], P('section'), may hold values from 0 to 2, as said below
Outputs:
- received: bfloat16 [32768, 18432], P('section', 'tp')
Inputs may be any that keep to these rules, and one draw needn't show every extreme that they name: `lengths`: the micro-batches fill the 4 blocks of 128 tokens in order; one spans 2 blocks and is full, each other fits one block. `evicted`: some section parks its micro-batch of 2 blocks and some section parks a micro-batch of one block. `kept_rows`: section i's own rows of the micro-batches it does not park, in buffer order, then unused rows. `parked_rows`: the rows that section i holds for its partner section: that section's parked micro-batch in buffer order, then unused rows.
All inputs are finite; a program needn't handle non-finite values.
Results may differ from a plain program's by a relative error of at most 0.0054.
Values may be sent and summed in bfloat16 or wider, within the bound.
No kernel may reach another device: no remote copies, remote signals or barrier semaphores. Data moves between devices by JAX's collectives and lax.ppermute only.
A program may use at most 128 MiB of HBM per device.

v0:
```python
import jax
import jax.numpy as jnp
from jax import lax
from jax.sharding import PartitionSpec as P

HD = 128
BLK = 128
MB = 3
NB = 4
PB = 2
KB = 3


def from_partner(shard, axis, stride):
    return lax.ppermute(shard, axis, [(i, i ^ 1 << stride) for i in range(lax.axis_size(axis))])


def passed_along(shard, axis, by):
    peers = lax.axis_size(axis)
    return lax.ppermute(shard, axis, [(i, (i + by) % peers) for i in range(peers)])


def layout_plan(lengths, evicted):
    counts = (lengths + BLK - 1) // BLK
    block_end = jnp.cumsum(counts)
    starts = block_end - counts
    blocks = jnp.arange(NB, dtype=jnp.int32)
    segment = jnp.sum((blocks[:, None] >= block_end[None, :]).astype(jnp.int32), axis=1)
    picked = jnp.arange(MB, dtype=jnp.int32) == evicted
    first_block = jnp.sum(jnp.where(picked, starts, 0))
    span_len = jnp.sum(jnp.where(picked, counts, 0))
    kept_index = blocks - jnp.where(blocks >= first_block + span_len, span_len, 0)
    source = jnp.where(segment == evicted, KB + blocks - first_block, kept_index)
    tok_owner = jnp.repeat(segment, BLK, total_repeat_length=NB * BLK)
    row_ids = jnp.arange(NB * BLK, dtype=jnp.int32)
    member = tok_owner[:, None] == jnp.arange(MB, dtype=jnp.int32)[None, :]
    offset = row_ids - BLK * jnp.sum(jnp.where(member, starts[None, :], 0), axis=1)
    inside = offset < jnp.sum(jnp.where(member, lengths[None, :], 0), axis=1)
    return (source, tok_owner, offset, inside)


def assemble(kept_rows, fetched, source):
    columns = kept_rows.shape[1]
    stacked = jnp.concatenate(
        [kept_rows.reshape(KB, BLK, columns), fetched.reshape(PB, BLK, columns)], axis=0
    )
    return jnp.take(stacked, source, axis=0).reshape(NB * BLK, columns)


def partner(panel_rows):
    section_count = lax.axis_size("section")
    return from_partner(panel_rows, "section", section_count.bit_length() - 2)


def backward(stash, out_grad, tok_owner, offset, inside):
    tokens = stash.shape[0]
    head_count = stash.shape[1] // (3 * HD)
    split = stash.reshape(tokens, head_count, 3, HD)
    queries, key_rows, value_rows = (split[:, :, 0], split[:, :, 1], split[:, :, 2])
    masked = jnp.where(inside[:, None], out_grad, jnp.zeros((), jnp.bfloat16))
    grad_rows = masked.reshape(tokens, head_count, HD)
    factor = HD ** (-0.5)
    scores = (
        jnp.einsum("qhd,khd->hqk", queries, key_rows, preferred_element_type=jnp.float32) * factor
    )
    allowed = (
        (tok_owner[:, None] == tok_owner[None, :])
        & (offset[None, :] <= offset[:, None])
        & inside[None, :]
    )
    scores = jnp.where(allowed[None], scores, -jnp.inf)
    row_max = jnp.max(scores, axis=-1, keepdims=True)
    raised = jnp.exp(scores - row_max)
    attend = raised / jnp.sum(raised, axis=-1, keepdims=True)
    attend_low = attend.astype(jnp.bfloat16)
    value_grad = jnp.einsum(
        "hqk,qhd->khd", attend_low, grad_rows, preferred_element_type=jnp.float32
    ).astype(jnp.bfloat16)
    prob_grad = jnp.einsum(
        "qhd,khd->hqk", grad_rows, value_rows, preferred_element_type=jnp.float32
    )
    row_dot = jnp.sum(attend * prob_grad, axis=-1, keepdims=True)
    score_grad = (attend * (prob_grad - row_dot)).astype(jnp.bfloat16)
    query_grad = (
        jnp.einsum("hqk,khd->qhd", score_grad, key_rows, preferred_element_type=jnp.float32)
        * factor
    ).astype(jnp.bfloat16)
    key_grad = (
        jnp.einsum("hqk,qhd->khd", score_grad, queries, preferred_element_type=jnp.float32) * factor
    ).astype(jnp.bfloat16)
    return jnp.stack([query_grad, key_grad, value_grad], axis=2).reshape(
        tokens, head_count * 3 * HD
    )


def shards(kept_rows, parked_rows, grad_out, lengths, evicted):
    relaid = lax.all_to_all(parked_rows, "tp", split_axis=1, concat_axis=0, tiled=True)
    fetched = partner(relaid)
    source, tok_owner, offset, inside = layout_plan(lengths, evicted[0])
    stash = assemble(kept_rows, fetched, source)
    gradient = backward(stash, grad_out, tok_owner, offset, inside)
    return passed_along(gradient, "section", -1)


def solution(mesh):
    in_specs = (
        P("section", "tp"),
        P(("section", "tp"), None),
        P("section", "tp"),
        P(),
        P("section"),
    )
    out_specs = P("section", "tp")
    return jax.shard_map(shards, mesh=mesh, in_specs=in_specs, out_specs=out_specs, check_vma=False)
```

profile of v0, /device:TPU:63, one launch (start us, length us, event | category | flops | bytes accessed | tf_op | source)
XLA Modules:
  0.0 249.7 jit_solution(10805003235502784554)
XLA Ops:
  0.0 3.4 %copy.70 = bf16[8,4,8,4608]{3,2,0,1:T(8,128)(2,1)} copy(bf16[8,4,8,4608]{3,2,1,0:T(8,128)(2,1)} %bitcast.74) | data formatting | bytes 4718592 | tf_op jit(solution)/shard_map/all_to_all | solution.py:97
  3.4 7.3 %all-to-all-start = ((bf16[64,4,4608]{2,0,1:T(8,128)(2,1)}), bf16[64,4,4608]{2,0,1:T(8,128)(2,1)}, u32[]{:S(2)}, u32[]{:S(2)}) async-start(bf16[64,4,4608]{2,0,1:T(8,128)(2,1)} %bitcast.67), calls=%async_computation | async-start | bytes 4718592 | tf_op jit(solution)/shard_map/all_to_all | solution.py:97
  12.2 0.7 fusion.19
  14.3 1.3 fusion.23
  15.6 50.7 %all-to-all-done = bf16[64,4,4608]{2,0,1:T(8,128)(2,1)} async-done(((bf16[64,4,4608]{2,0,1:T(8,128)(2,1)}), bf16[64,4,4608]{2,0,1:T(8,128)(2,1)}, u32[]{:S(2)}, u32[]{:S(2)}) %all-to-all-start) | async-done | bytes 2359328 | tf_op jit(solution)/shard_map/all_to_all | solution.py:97
  66.3 0.7 copy.50
  67.7 2.4 compare_select_fusion.1
  70.3 1.3 compare_and_fusion
  72.0 1.3 broadcast_select_fusion
  73.3 44.3 %collective-permute-done = bf16[256,4608]{1,0:T(8,128)(2,1)} collective-permute-done((bf16[256,4608]{1,0:T(8,128)(2,1)}, bf16[256,4608]{1,0:T(8,128)(2,1)}, u32[]{:S(2)}, u32[]{:S(2)}) %collective-permute-start) | collective-permute-done | bytes 2359328 | tf_op jit(solution)/shard_map/ppermute | solution.py:15
  117.6 5.7 %pad_maximum_fusion = bf16[5,128,4608]{2,1,0:T(8,128)(2,1)} fusion(bf16[2,128,4608]{2,1,0:T(8,128)(2,1)} %bitcast.7, bf16[3,128,4608]{2,1,0:T(8,128)(2,1)} %bitcast.73), kind=kLoop, calls=%fused_computation.13 | loop fusion | flops 2949120 | bytes 11796480 | tf_op jit(solution)/shard_map/concatenate | solution.py:44
  123.4 5.7 %gather_fusion = bf16[4,128,4608]{2,1,0:T(8,128)(2,1)} fusion(bf16[5,128,4608]{2,1,0:T(8,128)(2,1)} %pad_maximum_fusion, s32[1024]{0:T(1024)S(1)} %pad_clamp_fusion), kind=kCustom, calls=%fused_computation | custom fusion | bytes 9437200 | tf_op jit(solution)/shard_map/jit(_take)/gather | solution.py:47
  129.1 11.8 %reshape.341 = bf16[512,12,3,128]{3,2,1,0:T(4,128)(2,1)} reshape(bf16[4,128,4608]{2,1,0:T(8,128)(2,1)} %gather_fusion) | data formatting | bytes 9437184 | tf_op jit(solution)/shard_map/jit(_take)/gather | solution.py:47
  140.9 5.1 %copy_select_fusion = bf16[512,12,3,128]{3,0,1,2:T(8,128)(2,1)S(1)} fusion(bf16[512,12,3,128]{3,2,1,0:T(4,128)(2,1)} %reshape.341, pred[512]{0:T(512)(128)(4,1)S(1)} %broadcast_bitcast_fusion), kind=kLoop, calls=%fused_computation.15 | loop fusion | flops 2359296 | bytes 9437696 | tf_op jit(solution)/shard_map/jit(_take)/select_n | solution.py:47
  146.0 6.4 %fusion.16 = f32[12,512,512]{1,2,0:T(8,128)} fusion(bf16[512,12,3,128]{3,0,1,2:T(8,128)(2,1)S(1)} %copy_select_fusion), kind=kOutput, calls=%fused_computation.28 | convolution fusion | flops 805306368 | bytes 15728640 | tf_op jit(solution)/shard_map/qhd,khd->hqk/dot_general | solution.py:64
  152.4 10.8 %fusion.28 = (f32[12,512]{1,0:T(8,128)S(1)}, f32[12,512,512]{1,2,0:T(8,128)S(1)}) fusion(f32[12,512,512]{1,2,0:T(8,128)} %fusion.16, pred[512,512]{0,1:T(8,128)(4,1)S(1)} %and_and_fusion), kind=kOutput, calls=%fused_computation.70 | output fusion | flops 18874880 | bytes 25452544 | tf_op jit(solution)/shard_map/sub | solution.py:73
  163.2 4.9 %fusion.11 = bf16[512,12,1,128]{0,3,1,2:T(8,128)(2,1)} fusion(bf16[512,12,128]{0,2,1:T(8,128)(2,1)} %bitcast.75, f32[12,512,512]{1,2,0:T(8,128)S(1)} %get-tuple-element.28, f32[12,512]{1,0:T(8,128)S(1)} %get-tuple-element.27), kind=kOutput, calls=%fused_computation.25 | convolution fusion | flops 812384256 | bytes 15753216 | tf_op jit(solution)/shard_map/hqk,qhd->khd/dot_general | solution.py:76
  168.1 5.5 %multiply_reduce_fusion = (f32[12,512]{1,0:T(8,128)S(1)}, f32[12,512,512]{1,2,0:T(8,128)}) fusion(f32[12,512,512]{1,2,0:T(8,128)S(1)} %get-tuple-element.28, f32[12,512]{1,0:T(8,128)S(1)} %get-tuple-element.27, bf16[512,12,128]{0,2,1:T(8,128)(2,1)S(1)} %bitcast.76, bf16[512,12,3,128]{3,0,1,2:T(8,128)(2,1)S(1)} %copy_select_fusion), kind=kOutput, calls=%fused_computation.3 | convolution fusion | flops 814737408 | bytes 28368896 | tf_op jit(solution)/shard_map/qhd,khd->hqk/dot_general | solution.py:79
  173.6 6.8 %multiply_convert_fusion = bf16[12,512,512]{1,2,0:T(8,128)(2,1)S(1)} fusion(f32[12,512,512]{1,2,0:T(8,128)} %get-tuple-element.30, f32[12,512]{1,0:T(8,128)S(1)} %get-tuple-element.29, f32[12,512,512]{1,2,0:T(8,128)S(1)} %get-tuple-element.28, f32[12,512]{1,0:T(8,128)S(1)} %get-tuple-element.27), kind=kLoop, calls=%fused_computation.2 | loop fusion | flops 12582912 | bytes 31506432 | tf_op jit(solution)/shard_map/convert_element_type | solution.py:83
  180.4 2.3 fusion.15
  182.7 1.2 fusion.14
  185.2 2.8 %collective-permute-start.1 = (bf16[512,4608]{0,1:T(8,128)(2,1)S(1)}, bf16[512,4608]{0,1:T(8,128)(2,1)}, u32[]{:S(2)}, u32[]{:S(2)}) collective-permute-start(bf16[512,4608]{0,1:T(8,128)(2,1)S(1)} %bitcast.72), channel_id=1, source_target_pairs={{0,252},{4,0},{8,4},{12,8},{16,12},{20,16},{24,20},{28,24},{32,28}... | collective-permute-start | bytes 14155784 | tf_op jit(solution)/shard_map/ppermute | solution.py:20
  187.9 55.2 %collective-permute-done.1 = bf16[512,4608]{0,1:T(8,128)(2,1)} collective-permute-done((bf16[512,4608]{0,1:T(8,128)(2,1)S(1)}, bf16[512,4608]{0,1:T(8,128)(2,1)}, u32[]{:S(2)}, u32[]{:S(2)}) %collective-permute-start.1) | collective-permute-done | bytes 4718624 | tf_op jit(solution)/shard_map/ppermute | solution.py:20
  243.1 6.6 %copy.58 = bf16[512,4608]{1,0:T(8,128)(2,1)} copy(bf16[512,4608]{0,1:T(8,128)(2,1)} %collective-permute-done.1) | data formatting | bytes 9437184 | tf_op jit(solution)/shard_map/ppermute | solution.py:20
  (24 shorter events, 3.3 us)
Async XLA Ops:
  0.0 11.3 %copy-start.3 = (s32[3]{0:T(128)S(1)}, s32[3]{0:T(128)}, u32[]{:S(2)}) copy-start(s32[3]{0:T(128)} %param.10) | copy-start | bytes 40
  0.0 66.3 %copy-start.1 = (bf16[512,1536]{1,0:T(8,128)(2,1)S(1)}, bf16[512,1536]{1,0:T(8,128)(2,1)}, u32[]{:S(2)}) copy-start(bf16[512,1536]{1,0:T(8,128)(2,1)} %param.9) | copy-start | bytes 4718596
  3.4 62.9 %all-to-all-start = ((bf16[64,4,4608]{2,0,1:T(8,128)(2,1)}), bf16[64,4,4608]{2,0,1:T(8,128)(2,1)}, u32[]{:S(2)}, u32[]{:S(2)}) async-start(bf16[64,4,4608]{2,0,1:T(8,128)(2,1)} %bitcast.67), calls=%async_computation | async-start | bytes 4718592 | tf_op jit(solution)/shard_map/all_to_all | solution.py:97
  66.3 51.3 %collective-permute-start = (bf16[256,4608]{1,0:T(8,128)(2,1)}, bf16[256,4608]{1,0:T(8,128)(2,1)}, u32[]{:S(2)}, u32[]{:S(2)}) collective-permute-start(bf16[256,4608]{1,0:T(8,128)(2,1)} %bitcast.6), channel_id=1, source_target_pairs={{0,128},{4,132},{8,136},{12,140},{16,144},{20,148},{24,152},{28,15... | collective-permute-start | bytes 7077896 | tf_op jit(solution)/shard_map/ppermute | solution.py:15
  163.2 4.9 %copy-start.2 = (bf16[512,1536]{0,1:T(8,128)(2,1)S(1)}, bf16[512,1536]{0,1:T(8,128)(2,1)}, u32[]{:S(2)}) copy-start(bf16[512,1536]{0,1:T(8,128)(2,1)} %broadcast_select_fusion) | copy-start | bytes 4718596
  182.7 1.4 copy-start
  185.2 57.9 %collective-permute-start.1 = (bf16[512,4608]{0,1:T(8,128)(2,1)S(1)}, bf16[512,4608]{0,1:T(8,128)(2,1)}, u32[]{:S(2)}, u32[]{:S(2)}) collective-permute-start(bf16[512,4608]{0,1:T(8,128)(2,1)S(1)} %bitcast.72), channel_id=1, source_target_pairs={{0,252},{4,0},{8,4},{12,8},{16,12},{20,16},{24,20},{28,24},{32,28}... | collective-permute-start | bytes 14155784 | tf_op jit(solution)/shard_map/ppermute | solution.py:20
where the time goes:
time: 251 us; the launch traced here: 250 us
  waiting for transfers between devices  150 us (60%)
  other arithmetic  37.4 us (15%)
  local copies, waits for them, and re-layouts  29.7 us (12%)
  matrix products  20.3 us (8%)
  starting transfers between devices  10 us (4%)
    ppermute x1, waiting for transfers between devices, passed_along(): lax.ppermute(shard, axis, [(i, (i + by) % peers) for i in range(peers)])  55.2 us
    all_to_all x1, waiting for transfers between devices, shards(): lax.all_to_all(parked_rows, 'tp', split_axis=1, concat_axis=0, tiled=True)  50.7 us
    ppermute x1, waiting for transfers between devices, from_partner(): lax.ppermute(shard, axis, [(i, i ^ 1 << stride) for i in range(lax.axis_s...  44.3 us
    gather x2, local copies, waits for them, and re-layouts, assemble(): return jnp.take(stacked, source, axis=0).reshape(NB * BLK, columns)  17.5 us
    sub x1, other arithmetic, backward(): raised = jnp.exp(scores - row_max)  10.8 us
    all_to_all x1, starting transfers between devices, shards(): lax.all_to_all(parked_rows, 'tp', split_axis=1, concat_axis=0, tiled=True)  7.28 us
    convert_element_type x1, other arithmetic, backward(): score_grad = (attend * (prob_grad - row_dot)).astype(jnp.bfloat16)  6.8 us
    ppermute x1, local copies, waits for them, and re-layouts, passed_along(): lax.ppermute(shard, axis, [(i, (i + by) % peers) for i in range(peers)])  6.61 us
  transfers between devices with their start and end apart: 3, of which 3 were waited for; matrix products, arithmetic and copies ran while one was open for 4% of the time, Pallas kernels for 0%

commit v1 on v0

v1 whole, which is shorter than its diff:
```python
import functools

import jax
import jax.numpy as jnp
from jax import lax
from jax.experimental import pallas as pl
from jax.experimental.pallas import tpu as pltpu
from jax.sharding import PartitionSpec as P

HD = 128
BLK = 128
KB = 3
HW = 3 * HD
FACTOR = HD**-0.5
PER_STEP = 2
HOPS = (3, -3, 1, -1)
KEPT_CHUNKS = (6, 6)
KEPT_COST = 300_000_000
PARKED_COST = 300_000_000
PARKED_CHUNKS = (6, 6)


def pick(index, values):
    return jnp.where(index == 0, values[0], jnp.where(index == 1, values[1], values[2]))


class Plan:
    def __init__(self, lengths, evicted):
        self.lengths = [lengths[m] for m in range(3)]
        counts = [lax.shift_right_logical(n + (BLK - 1), 7) for n in self.lengths]
        self.starts = [jnp.int32(0), counts[0], counts[0] + counts[1]]
        which = evicted[0]
        self.first = pick(which, self.starts)
        self.span = pick(which, counts)
        self.long = self.span > 1

    def segment(self, block):
        return (block >= self.starts[1]).astype(jnp.int32) + (block >= self.starts[2]).astype(jnp.int32)

    def valid(self, block):
        m = self.segment(block)
        return jnp.clip(pick(m, self.lengths) - BLK * (block - pick(m, self.starts)), 0, BLK)

    def kept(self, slot):
        return jnp.minimum(slot + jnp.where(slot >= self.first, self.span, 0), 3)

    def parked(self, slot):
        return jnp.minimum(self.first + slot, 3)

    def late(self, slot):
        return jnp.where(slot == 0, self.first, jnp.where(self.long, self.parked(1), self.kept(2)))


def nt(a, b):
    return lax.dot_general(a, b, (((1,), (1,)), ((), ())), preferred_element_type=jnp.float32)


def nn(a, b):
    return lax.dot_general(a, b, (((1,), (0,)), ((), ())), preferred_element_type=jnp.float32)


def tn(a, b):
    return lax.dot_general(a, b, (((0,), (0,)), ((), ())), preferred_element_type=jnp.float32)


def attention_grads(q, k, v, grads, valids, joins):
    count = len(q)
    key_ids = lax.broadcasted_iota(jnp.int32, (BLK, BLK), 0)
    query_ids = lax.broadcasted_iota(jnp.int32, (BLK, BLK), 1)
    dq, dk, dv = [None] * count, [None] * count, [None] * count
    for j in range(count):
        grad = jnp.where(key_ids < valids[j], grads[j], jnp.zeros((), jnp.bfloat16))
        allowed = (key_ids <= query_ids) & (key_ids < valids[j])
        if j == 0:
            keys, values = k[0], v[0]
        else:
            keys, values = jnp.concatenate([k[j - 1], k[j]]), jnp.concatenate([v[j - 1], v[j]])
            before = jnp.broadcast_to(joins[j], (BLK, BLK))
            allowed = jnp.concatenate([before, allowed])
        scores = jnp.where(allowed, nt(keys, q[j]) * FACTOR, -jnp.inf)
        raised = jnp.exp(scores - jnp.max(scores, axis=0, keepdims=True))
        attend = raised * (1.0 / jnp.sum(raised, axis=0, keepdims=True))
        prob_grad = nt(values, grad)
        row_dot = jnp.sum(attend * prob_grad, axis=0, keepdims=True)
        score_grad = (attend * (prob_grad - row_dot)).astype(jnp.bfloat16)
        value_part = nn(attend.astype(jnp.bfloat16), grad)
        key_part = nn(score_grad, q[j])
        dq[j] = tn(score_grad, keys)
        if j == 0:
            dk[0], dv[0] = key_part, value_part
        else:
            dk[j - 1], dv[j - 1] = dk[j - 1] + key_part[:BLK], dv[j - 1] + value_part[:BLK]
            dk[j], dv[j] = key_part[BLK:], value_part[BLK:]
    low = lambda x: x.astype(jnp.bfloat16)
    return [low(x * FACTOR) for x in dq], [low(x * FACTOR) for x in dk], [low(x) for x in dv]


def worth(flops):
    return pl.CostEstimate(flops=flops, bytes_accessed=1 << 20, transcendentals=0)


def columns(head, part):
    return slice(head * HW + part * HD, head * HW + (part + 1) * HD)


def kept_kernel(lengths, evicted, rows, g0, g1, g2, early, third):
    plan = Plan(lengths, evicted)
    blocks = [plan.kept(j) for j in range(KB)]
    valids = [plan.valid(b) for b in blocks]
    segments = [plan.segment(b) for b in blocks]
    joins = [None] + [(segments[j] == segments[j - 1]) & jnp.logical_not(plan.long) for j in range(1, KB)]
    for head in range(PER_STEP):
        q, k, v = ([rows[j * BLK : (j + 1) * BLK, columns(head, p)] for j in range(KB)] for p in range(3))
        grads = [g[:, head * HD : (head + 1) * HD] for g in (g0, g1, g2)]
        for part, made in enumerate(attention_grads(q, k, v, grads, valids, joins)):
            early[0:BLK, columns(head, part)] = made[0]
            early[BLK : 2 * BLK, columns(head, part)] = made[1]
            third[:, columns(head, part)] = made[2]


def kept_part(lengths, evicted, kept_rows, grad_out, first, heads):
    at = first // PER_STEP
    grad_spec = lambda j: pl.BlockSpec(
        (BLK, PER_STEP * HD), lambda i, ln, ev: (Plan(ln, ev).kept(j), at + i)
    )
    return pl.pallas_call(
        kept_kernel,
        grid_spec=pltpu.PrefetchScalarGridSpec(
            num_scalar_prefetch=2,
            grid=(heads // PER_STEP,),
            in_specs=[pl.BlockSpec((KB * BLK, PER_STEP * HW), lambda i, ln, ev: (0, at + i))]
            + [grad_spec(j) for j in range(KB)],
            out_specs=[
                pl.BlockSpec((2 * BLK, PER_STEP * HW), lambda i, ln, ev: (0, i)),
                pl.BlockSpec((BLK, PER_STEP * HW), lambda i, ln, ev: (0, i)),
            ],
        ),
        out_shape=[
            jax.ShapeDtypeStruct((2 * BLK, heads * HW), jnp.bfloat16),
            jax.ShapeDtypeStruct((BLK, heads * HW), jnp.bfloat16),
        ],
        compiler_params=pltpu.CompilerParams(vmem_limit_bytes=32 << 20),
        cost_estimate=worth(heads * KEPT_COST),
        name="kept_grads",
    )(lengths, evicted, kept_rows, grad_out, grad_out, grad_out)


def parked_kernel(lengths, evicted, quarters, r0, r1, r2, r3, g0, g1, third, late, rows):
    plan = Plan(lengths, evicted)
    quarter = BLK // 2
    for d, piece in enumerate((r0, r1, r2, r3)):
        start = pl.multiple_of(quarters[d] * quarter, quarter)
        rows[pl.ds(start, quarter), :] = piece[...]
    valids = [plan.valid(plan.parked(j)) for j in range(2)]
    joins = [None, plan.long]
    for head in range(PER_STEP):
        q, k, v = ([rows[j * BLK : (j + 1) * BLK, columns(head, p)] for j in range(2)] for p in range(3))
        grads = [g[:, head * HD : (head + 1) * HD] for g in (g0, g1)]
        grads[1] = jnp.where(plan.long, grads[1], jnp.zeros((), jnp.bfloat16))
        for part, made in enumerate(attention_grads(q, k, v, grads, valids, joins)):
            late[0:BLK, columns(head, part)] = made[0]
            late[BLK : 2 * BLK, columns(head, part)] = jnp.where(
                plan.long, made[1], third[:, columns(head, part)]
            )


def parked_part(lengths, evicted, quarters, pieces, grad_out, third, third_at, first, heads):
    at = first // PER_STEP
    third_at = third_at // PER_STEP
    grad_spec = lambda j: pl.BlockSpec(
        (BLK, PER_STEP * HD), lambda i, ln, ev, sh: (Plan(ln, ev).parked(j), at + i)
    )
    return pl.pallas_call(
        parked_kernel,
        grid_spec=pltpu.PrefetchScalarGridSpec(
            num_scalar_prefetch=3,
            grid=(heads // PER_STEP,),
            in_specs=[pl.BlockSpec((BLK // 2, PER_STEP * HW), lambda i, ln, ev, sh: (0, i))] * 4
            + [grad_spec(j) for j in range(2)]
            + [pl.BlockSpec((BLK, PER_STEP * HW), lambda i, ln, ev, sh: (0, third_at + i))],
            out_specs=pl.BlockSpec((2 * BLK, PER_STEP * HW), lambda i, ln, ev, sh: (0, i)),
            scratch_shapes=[pltpu.VMEM((2 * BLK, PER_STEP * HW), jnp.bfloat16)],
        ),
        out_shape=jax.ShapeDtypeStruct((2 * BLK, heads * HW), jnp.bfloat16),
        compiler_params=pltpu.CompilerParams(vmem_limit_bytes=32 << 20),
        cost_estimate=worth(heads * PARKED_COST),
        name="parked_grads",
    )(lengths, evicted, quarters, *pieces, grad_out, grad_out, third)


def place_kernel(slot_of, first, lengths, evicted, piece, *refs):
    out, sems = refs[-2:]
    plan = Plan(lengths, evicted)
    copies = []
    for slot in range(2):
        start = pl.multiple_of(slot_of(plan, slot) * BLK, BLK)
        copies.append(
            pltpu.make_async_copy(
                piece.at[pl.ds(slot * BLK, BLK), :],
                out.at[pl.ds(start, BLK), pl.ds(first * HW, piece.shape[1])],
                sems.at[slot],
            )
        )
    for copy in copies:
        copy.start()
    for copy in copies:
        copy.wait()


def place(lengths, evicted, piece, out, slot_of, first, total):
    base = (lengths, evicted, piece) if out is None else (lengths, evicted, piece, out)
    smem, vmem, hbm = (pl.BlockSpec(memory_space=m) for m in (pltpu.SMEM, pltpu.VMEM, pl.ANY))
    return pl.pallas_call(
        functools.partial(place_kernel, slot_of, first),
        in_specs=[smem, smem, vmem] + [hbm] * (len(base) - 3),
        out_specs=hbm,
        scratch_shapes=[pltpu.SemaphoreType.DMA((2,))],
        out_shape=jax.ShapeDtypeStruct(total, jnp.bfloat16),
        input_output_aliases={} if out is None else {3: 0},
        name="place_rows",
    )(*base)


def shards(kept_rows, parked_rows, grad_out, lengths, evicted):
    sections, peers = lax.axis_size("section"), lax.axis_size("tp")
    half = sections // 2
    ring = 2 * peers
    total = (grad_out.shape[0], kept_rows.shape[1])
    share = total[1]
    spot = 2 * lax.axis_index("tp") + lax.axis_index("section") // half

    def shifted(rows, hops):
        pairs = []
        for s in range(sections):
            for t in range(peers):
                to = (2 * t + s // half + hops) % ring
                pairs.append((s * peers + t, ((s + half) % sections) * peers + to // 2))
        return lax.ppermute(rows, ("section", "tp"), pairs)

    def passed_back(rows):
        return lax.ppermute(rows, "section", [(i, (i - 1) % sections) for i in range(sections)])

    next_evicted = passed_back(evicted)

    arrived = []
    first = 0
    for heads in PARKED_CHUNKS:
        width = heads * HW
        pieces = []
        for hops in HOPS:
            to = lax.rem(spot + hops + ring, ring) // 2
            rows = lax.dynamic_slice(parked_rows, (0, to * share + first * HW), (parked_rows.shape[0], width))
            pieces.append(shifted(rows, hops))
        arrived.append(pieces)
        first += heads
    quarters = jnp.stack([lax.rem(spot - hops + ring, ring) // 2 for hops in HOPS]).astype(jnp.int32)

    out = None
    thirds = []
    received = []
    first = 0

    def after(rows):
        return passed_back(rows)

    for heads in KEPT_CHUNKS:
        early, third = kept_part(lengths, evicted, kept_rows, grad_out, first, heads)
        thirds.append((first, heads, third))
        received.append((after(early), Plan.kept, first))
        first += heads

    first = 0
    for heads, pieces in zip(PARKED_CHUNKS, arrived):
        at, third = next((f, t) for f, n, t in thirds if f <= first and first + heads <= f + n)
        late = parked_part(lengths, evicted, quarters, pieces, grad_out, third, first - at, first, heads)
        received.append((after(late), Plan.late, first))
        first += heads

    for piece, slot_of, first in received:
        out = place(lengths, next_evicted, piece, out, slot_of, first, total)
    return out


def solution(mesh):
    in_specs = (
        P("section", "tp"),
        P(("section", "tp"), None),
        P("section", "tp"),
        P(),
        P("section"),
    )
    out_specs = P("section", "tp")
    return jax.shard_map(shards, mesh=mesh, in_specs=in_specs, out_specs=out_specs, check_vma=False)
```

time: 251 us -> 125 us (0.50)
  waiting for transfers between devices: 150 us -> 63.7 us
  other arithmetic: 37.4 us -> 0.08 us
  Pallas kernels: 0 us -> 36 us
  local copies, waits for them, and re-layouts: 29.7 us -> 3.86 us
  matrix products: 20.3 us -> 0 us
  starting transfers between devices: 10 us -> 19.7 us
    all_to_all x1 -> x0, waiting for transfers between devices: 50.7 us -> none  [shards(): lax.all_to_all(parked_rows, 'tp', split_axis=1, concat_axis=0, tiled=True)]
    pallas_call x0 -> x8, Pallas kernels: none -> 36 us  [the longest x2 13.5 us: kept_part(): pl.pallas_call(kept_kernel, grid_spec=pltpu.PrefetchScalarGridSpec(num_sc...]
    ppermute x2 -> x13, waiting for transfers between devices: 99.5 us -> 63.7 us  [the longest x5 42.6 us: passed_back(): lax.ppermute(rows, 'section', [(i, (i - 1) % sections) for i in range(sec...]
    dot_general x5 -> x0, matrix products: 20.3 us -> none  [the longest x1 6.37 us: backward(): jnp.einsum('qhd,khd->hqk', queries, key_rows, preferred_element_type=jnp....]
    gather x3 -> x0, local copies, waits for them, and re-layouts: 18.2 us -> none  [the longest x2 17.5 us: assemble(): return jnp.take(stacked, source, axis=0).reshape(NB * BLK, columns)]
    ppermute x2 -> x13, starting transfers between devices: 2.77 us -> 19.7 us  [the longest x8 10.8 us: shifted(): return lax.ppermute(rows, ('section', 'tp'), pairs)]
    sub x3 -> x0, other arithmetic: 10.8 us -> none  [the longest x1 10.8 us: backward(): raised = jnp.exp(scores - row_max)]
    select_n x4 -> x0, other arithmetic: 7.72 us -> none  [the longest x2 6.41 us: assemble(): return jnp.take(stacked, source, axis=0).reshape(NB * BLK, columns)]
  transfers between devices with their start and end apart: 3 -> 13, of which waited for: 3 -> 5; matrix products, arithmetic and copies ran while one was open for 4% -> 0% of each run, Pallas kernels for 0% -> 27%
where the time goes in v1:
time: 125 us; the launch traced here: 124 us
  waiting for transfers between devices  63.7 us (51%)
  Pallas kernels  36 us (29%)
  starting transfers between devices  19.7 us (16%)
  local copies, waits for them, and re-layouts  3.86 us (3%)
    ppermute x5, waiting for transfers between devices, passed_back(): lax.ppermute(rows, 'section', [(i, (i - 1) % sections) for i in range(sec...  42.6 us
    ppermute x8, waiting for transfers between devices, shifted(): return lax.ppermute(rows, ('section', 'tp'), pairs)  21 us
    pallas_call x2, Pallas kernels, kept_part(): pl.pallas_call(kept_kernel, grid_spec=pltpu.PrefetchScalarGridSpec(num_sc...  13.5 us
    pallas_call x4, Pallas kernels, place(): pl.pallas_call(functools.partial(place_kernel, slot_of, first), in_specs=...  11.5 us
    pallas_call x2, Pallas kernels, parked_part(): pl.pallas_call(parked_kernel, grid_spec=pltpu.PrefetchScalarGridSpec(num_...  10.9 us
    ppermute x8, starting transfers between devices, shifted(): return lax.ppermute(rows, ('section', 'tp'), pairs)  10.8 us
    ppermute x5, starting transfers between devices, passed_back(): lax.ppermute(rows, 'section', [(i, (i - 1) % sections) for i in range(sec...  8.96 us
  transfers between devices with their start and end apart: 13, of which 5 were waited for; matrix products, arithmetic and copies ran while one was open for 0% of the time, Pallas kernels for 27%

profile of v1, /device:TPU:63, one launch (start us, length us, event | category | flops | bytes accessed | tf_op | source)
XLA Modules:
  0.0 124.3 jit_solution(3721435243541498219)
XLA Ops:
  0.0 1.9 %constant_dynamic-slice_fusion = (bf16[64,2304]{1,0:T(8,128)(2,1)S(1)}, bf16[64,2304]{1,0:T(8,128)(2,1)S(1)}, bf16[64,2304]{1,0:T(8,128)(2,1)S(1)}, bf16[64,2304...) fusion(bf16[64,18432]{1,0:T(8,128)(2,1)} %param.6, ...), kind=kLoop, calls=%fused_computation | loop fusion | bytes 4718624 | tf_op jit(solution)/shard_map/dynamic_slice | solution.py:252
  1.9 0.1 collective-permute-start.9
  2.0 6.3 %collective-permute-start.7 = (bf16[64,2304]{1,0:T(8,128)(2,1)S(1)}, bf16[64,2304]{1,0:T(8,128)(2,1)S(1)}, u32[]{:S(2)}, u32[]{:S(2)}) collective-permute-start(bf16[64,2304]{1,0:T(8,128)(2,1)S(1)} %get-tuple-element.14), channel_id=1, source_target_pairs={{0,130},{1,131},{2,128},{3,129},{4,134},{5,135},{6,132},{7,133},{8... | collective-permute-start | bytes 884744 | tf_op jit(solution)/shard_map/ppermute | solution.py:238
  8.2 2.4 %collective-permute-start.4 = (bf16[64,2304]{1,0:T(8,128)(2,1)S(1)}, bf16[64,2304]{1,0:T(8,128)(2,1)S(1)}, u32[]{:S(2)}, u32[]{:S(2)}) collective-permute-start(bf16[64,2304]{1,0:T(8,128)(2,1)S(1)} %get-tuple-element.16), channel_id=1, source_target_pairs={{0,131},{1,128},{2,129},{3,130},{4,135},{5,132},{6,133},{7,134},{8... | collective-permute-start | bytes 884744 | tf_op jit(solution)/shard_map/ppermute | solution.py:238
  11.3 2.0 %copy-done.1 = bf16[384,4608]{1,0:T(8,128)(2,1)S(1)} copy-done((bf16[384,4608]{1,0:T(8,128)(2,1)S(1)}, bf16[384,4608]{1,0:T(8,128)(2,1)}, u32[]{:S(2)}) %copy-start.1) | copy-done | bytes 3538968
  13.3 6.8 %kept_grads.3 = (bf16[256,2304]{1,0:T(8,128)(2,1)S(1)}, bf16[128,2304]{1,0:T(8,128)(2,1)S(1)}) custom-call(s32[3]{0:T(128)S(1)} %copy-done.2, s32[1]{0:T(128)S(6)} %copy.12.evicted, bf16[384,4608]{1,0:T(8,128)(2,1)S(1)} %copy-done.1, bf16[512,1536]{1,0:T(8,128)(2,1)S(1)} %copy-done, bf16[512,1536]{1,0:T(8,128)(2,1)S(1)} %copy-done, bf16[512,1536]{1,0:T(8,128)(2,1)S(1)} %copy-done), custom_call_target="tpu_custom_call" | custom-call | flops 1800000000 | bytes 1048576 | tf_op jit(solution)/shard_map/kept_grads/pallas_call | solution.py:126
  20.2 7.9 %collective-permute-done.7.r1 = bf16[64,2304]{1,0:T(8,128)(2,1)S(1)} collective-permute-done((bf16[64,2304]{1,0:T(8,128)(2,1)S(1)}, bf16[64,2304]{1,0:T(8,128)(2,1)S(1)}, u32[]{:S(2)}, u32[]{:S(2)}) %collective-permute-start.7) | collective-permute-done | bytes 294944 | tf_op jit(solution)/shard_map/ppermute | solution.py:238
  28.1 2.5 %collective-permute-done.6.r0 = bf16[64,2304]{1,0:T(8,128)(2,1)S(1)} collective-permute-done((bf16[64,2304]{1,0:T(8,128)(2,1)S(1)}, bf16[64,2304]{1,0:T(8,128)(2,1)S(1)}, u32[]{:S(2)}, u32[]{:S(2)}) %collective-permute-start.6) | collective-permute-done | bytes 294944 | tf_op jit(solution)/shard_map/ppermute | solution.py:238
  30.6 2.0 %collective-permute-start.1 = (bf16[64,2304]{1,0:T(8,128)(2,1)S(1)}, bf16[64,2304]{1,0:T(8,128)(2,1)S(1)}, u32[]{:S(2)}, u32[]{:S(2)}) collective-permute-start(bf16[64,2304]{1,0:T(8,128)(2,1)S(1)} %get-tuple-element.19), channel_id=1, source_target_pairs={{0,129},{1,130},{2,131},{3,128},{4,133},{5,134},{6,135},{7,132},{8... | collective-permute-start | bytes 884744 | tf_op jit(solution)/shard_map/ppermute | solution.py:238
  32.5 6.8 %kept_grads.2 = (bf16[256,2304]{1,0:T(8,128)(2,1)S(1)}, bf16[128,2304]{1,0:T(8,128)(2,1)S(1)}) custom-call(s32[3]{0:T(128)S(1)} %copy-done.2, s32[1]{0:T(128)S(6)} %copy.12.evicted, bf16[384,4608]{1,0:T(8,128)(2,1)S(1)} %copy-done.1, bf16[512,1536]{1,0:T(8,128)(2,1)S(1)} %copy-done, bf16[512,1536]{1,0:T(8,128)(2,1)S(1)} %copy-done, bf16[512,1536]{1,0:T(8,128)(2,1)S(1)} %copy-done), custom_call_target="tpu_custom_call" | custom-call | flops 1800000000 | bytes 1048576 | tf_op jit(solution)/shard_map/kept_grads/pallas_call | solution.py:126
  39.4 5.9 %collective-permute-start.12 = (bf16[256,2304]{1,0:T(8,128)(2,1)S(1)}, bf16[256,2304]{1,0:T(8,128)(2,1)}, u32[]{:S(2)}, u32[]{:S(2)}) collective-permute-start(bf16[256,2304]{1,0:T(8,128)(2,1)S(1)} %get-tuple-element.12), channel_id=1, source_target_pairs={{0,252},{4,0},{8,4},{12,8},{16,12},{20,16},{24,20},{28,24},{32,28}... | collective-permute-start | bytes 3538952 | tf_op jit(solution)/shard_map/ppermute | solution.py:241
  45.3 5.5 %parked_grads.3 = bf16[256,2304]{1,0:T(8,128)(2,1)S(1)} custom-call(s32[3]{0:T(128)S(1)} %copy-done.2, s32[1]{0:T(128)S(6)} %copy.12.evicted, s32[4]{0:T(128)S(1)} %pad_add_fusion.quarters, bf16[64,2304]{1,0:T(8,128)(2,1)S(1)} %collective-permute-done.6.r0, bf16[64,2304]{1,0:T(8,128)(2,1)S(1)} %collective-permute-done.7.r1, ...), custom_call_target="tpu_custom_call" | custom-call | flops 1800000000 | bytes 1048576 | tf_op jit(solution)/shard_map/parked_grads/pallas_call | solution.py:173
  50.8 0.3 collective-permute-start.11
  51.1 0.9 collective-permute-start.10
  52.0 2.2 %collective-permute-done.2.r1 = bf16[64,2304]{1,0:T(8,128)(2,1)S(1)} collective-permute-done((bf16[64,2304]{1,0:T(8,128)(2,1)S(1)}, bf16[64,2304]{1,0:T(8,128)(2,1)S(1)}, u32[]{:S(2)}, u32[]{:S(2)}) %collective-permute-start.2) | collective-permute-done | bytes 294944 | tf_op jit(solution)/shard_map/ppermute | solution.py:238
  54.2 8.4 %collective-permute-done.1.r0 = bf16[64,2304]{1,0:T(8,128)(2,1)S(1)} collective-permute-done((bf16[64,2304]{1,0:T(8,128)(2,1)S(1)}, bf16[64,2304]{1,0:T(8,128)(2,1)S(1)}, u32[]{:S(2)}, u32[]{:S(2)}) %collective-permute-start.1) | collective-permute-done | bytes 294944 | tf_op jit(solution)/shard_map/ppermute | solution.py:238
  62.6 5.5 %parked_grads.2 = bf16[256,2304]{1,0:T(8,128)(2,1)S(1)} custom-call(s32[3]{0:T(128)S(1)} %copy-done.2, s32[1]{0:T(128)S(6)} %copy.12.evicted, s32[4]{0:T(128)S(1)} %pad_add_fusion.quarters, bf16[64,2304]{1,0:T(8,128)(2,1)S(1)} %collective-permute-done.1.r0, bf16[64,2304]{1,0:T(8,128)(2,1)S(1)} %collective-permute-done.2.r1, ...), custom_call_target="tpu_custom_call" | custom-call | flops 1800000000 | bytes 1048576 | tf_op jit(solution)/shard_map/parked_grads/pallas_call | solution.py:173
  68.1 1.7 %collective-permute-start.5 = (bf16[256,2304]{1,0:T(8,128)(2,1)S(1)}, bf16[256,2304]{1,0:T(8,128)(2,1)}, u32[]{:S(2)}, u32[]{:S(2)}) collective-permute-start(bf16[256,2304]{1,0:T(8,128)(2,1)S(1)} %parked_grads.2), channel_id=1, source_target_pairs={{0,252},{4,0},{8,4},{12,8},{16,12},{20,16},{24,20},{28,24},{32,28}... | collective-permute-start | bytes 3538952 | tf_op jit(solution)/shard_map/ppermute | solution.py:241
  69.8 0.1 collective-permute-start
  69.9 42.6 %collective-permute-done.evicted = s32[1]{0:T(128)} collective-permute-done((s32[1]{0:T(128)}, s32[1]{0:T(128)}, u32[]{:S(2)}, u32[]{:S(2)}) %collective-permute-start) | collective-permute-done | bytes 36 | tf_op jit(solution)/shard_map/ppermute | solution.py:241
  112.5 2.9 %place_rows.4.refs_0_ = bf16[512,4608]{1,0:T(8,128)(2,1)} custom-call(s32[3]{0:T(128)} %lengths.15, s32[1]{0:T(128)} %collective-permute-done.evicted, bf16[256,2304]{1,0:T(8,128)(2,1)} %collective-permute-done.12.piece), custom_call_target="tpu_custom_call" | custom-call | tf_op jit(solution)/shard_map/place_rows/pallas_call | solution.py:213
  115.4 2.9 %place_rows.5.refs_0_ = bf16[512,4608]{1,0:T(8,128)(2,1)} custom-call(s32[3]{0:T(128)} %lengths.15, s32[1]{0:T(128)} %collective-permute-done.evicted, bf16[256,2304]{1,0:T(8,128)(2,1)} %collective-permute-done.11.piece, bf16[512,4608]{1,0:T(8,128)(2,1)} %place_rows.4.refs_0_), custom_call_target="tpu_custom_call", output_to_operand_aliasing={{}: (3, {})} | custom-call | tf_op jit(solution)/shard_map/place_rows/pallas_call | solution.py:213
  118.3 2.9 %place_rows.6.refs_0_ = bf16[512,4608]{1,0:T(8,128)(2,1)} custom-call(s32[3]{0:T(128)} %lengths.15, s32[1]{0:T(128)} %collective-permute-done.evicted, bf16[256,2304]{1,0:T(8,128)(2,1)} %collective-permute-done.10.piece, bf16[512,4608]{1,0:T(8,128)(2,1)} %place_rows.5.refs_0_), custom_call_target="tpu_custom_call", output_to_operand_aliasing={{}: (3, {})} | custom-call | tf_op jit(solution)/shard_map/place_rows/pallas_call | solution.py:213
  121.2 2.9 %place_rows.7 = bf16[512,4608]{1,0:T(8,128)(2,1)} custom-call(s32[3]{0:T(128)} %lengths.15, s32[1]{0:T(128)} %collective-permute-done.evicted, bf16[256,2304]{1,0:T(8,128)(2,1)} %collective-permute-done.5.piece, bf16[512,4608]{1,0:T(8,128)(2,1)} %place_rows.6.refs_0_), custom_call_target="tpu_custom_call", output_to_operand_aliasing={{}: (3, {})} | custom-call | tf_op jit(solution)/shard_map/place_rows/pallas_call | solution.py:213
  (18 shorter events, 0.2 us)
Async XLA Ops:
  0.0 11.3 %copy-start = (bf16[512,1536]{1,0:T(8,128)(2,1)S(1)}, bf16[512,1536]{1,0:T(8,128)(2,1)}, u32[]{:S(2)}) copy-start(bf16[512,1536]{1,0:T(8,128)(2,1)} %g1.7) | copy-start | bytes 4718596
  0.0 11.3 %copy-start.2 = (s32[3]{0:T(128)S(1)}, s32[3]{0:T(128)}, u32[]{:S(2)}) copy-start(s32[3]{0:T(128)} %lengths.15) | copy-start | bytes 40
  1.9 18.2 %collective-permute-start.9 = (bf16[64,2304]{1,0:T(8,128)(2,1)S(1)}, bf16[64,2304]{1,0:T(8,128)(2,1)S(1)}, u32[]{:S(2)}, u32[]{:S(2)}) collective-permute-start(bf16[64,2304]{1,0:T(8,128)(2,1)S(1)} %get-tuple-element.13), channel_id=1, source_target_pairs={{0,131},{1,128},{2,129},{3,130},{4,135},{5,132},{6,133},{7,134},{8... | collective-permute-start | bytes 884744 | tf_op jit(solution)/shard_map/ppermute | solution.py:238
  2.0 26.1 %collective-permute-start.7 = (bf16[64,2304]{1,0:T(8,128)(2,1)S(1)}, bf16[64,2304]{1,0:T(8,128)(2,1)S(1)}, u32[]{:S(2)}, u32[]{:S(2)}) collective-permute-start(bf16[64,2304]{1,0:T(8,128)(2,1)S(1)} %get-tuple-element.14), channel_id=1, source_target_pairs={{0,130},{1,131},{2,128},{3,129},{4,134},{5,135},{6,132},{7,133},{8... | collective-permute-start | bytes 884744 | tf_op jit(solution)/shard_map/ppermute | solution.py:238
  8.2 22.3 %collective-permute-start.6 = (bf16[64,2304]{1,0:T(8,128)(2,1)S(1)}, bf16[64,2304]{1,0:T(8,128)(2,1)S(1)}, u32[]{:S(2)}, u32[]{:S(2)}) collective-permute-start(bf16[64,2304]{1,0:T(8,128)(2,1)S(1)} %get-tuple-element.15), channel_id=1, source_target_pairs={{0,129},{1,130},{2,131},{3,128},{4,133},{5,134},{6,135},{7,132},{8... | collective-permute-start | bytes 884744 | tf_op jit(solution)/shard_map/ppermute | solution.py:238
  8.2 42.6 %collective-permute-start.4 = (bf16[64,2304]{1,0:T(8,128)(2,1)S(1)}, bf16[64,2304]{1,0:T(8,128)(2,1)S(1)}, u32[]{:S(2)}, u32[]{:S(2)}) collective-permute-start(bf16[64,2304]{1,0:T(8,128)(2,1)S(1)} %get-tuple-element.16), channel_id=1, source_target_pairs={{0,131},{1,128},{2,129},{3,130},{4,135},{5,132},{6,133},{7,134},{8... | collective-permute-start | bytes 884744 | tf_op jit(solution)/shard_map/ppermute | solution.py:238
  10.6 28.8 %collective-permute-start.8 = (bf16[64,2304]{1,0:T(8,128)(2,1)S(1)}, bf16[64,2304]{1,0:T(8,128)(2,1)S(1)}, u32[]{:S(2)}, u32[]{:S(2)}) collective-permute-start(bf16[64,2304]{1,0:T(8,128)(2,1)S(1)} %get-tuple-element.20), channel_id=1, source_target_pairs={{0,128},{1,129},{2,130},{3,131},{4,132},{5,133},{6,134},{7,135},{8... | collective-permute-start | bytes 884744 | tf_op jit(solution)/shard_map/ppermute | solution.py:238
  11.3 2.0 %copy-start.1 = (bf16[384,4608]{1,0:T(8,128)(2,1)S(1)}, bf16[384,4608]{1,0:T(8,128)(2,1)}, u32[]{:S(2)}) copy-start(bf16[384,4608]{1,0:T(8,128)(2,1)} %rows.3) | copy-start | bytes 10616836
  20.1 31.0 %collective-permute-start.3 = (bf16[64,2304]{1,0:T(8,128)(2,1)S(1)}, bf16[64,2304]{1,0:T(8,128)(2,1)S(1)}, u32[]{:S(2)}, u32[]{:S(2)}) collective-permute-start(bf16[64,2304]{1,0:T(8,128)(2,1)S(1)} %get-tuple-element.17), channel_id=1, source_target_pairs={{0,128},{1,129},{2,130},{3,131},{4,132},{5,133},{6,134},{7,135},{8... | collective-permute-start | bytes 884744 | tf_op jit(solution)/shard_map/ppermute | solution.py:238
  28.1 26.1 %collective-permute-start.2 = (bf16[64,2304]{1,0:T(8,128)(2,1)S(1)}, bf16[64,2304]{1,0:T(8,128)(2,1)S(1)}, u32[]{:S(2)}, u32[]{:S(2)}) collective-permute-start(bf16[64,2304]{1,0:T(8,128)(2,1)S(1)} %get-tuple-element.18), channel_id=1, source_target_pairs={{0,130},{1,131},{2,128},{3,129},{4,134},{5,135},{6,132},{7,133},{8... | collective-permute-start | bytes 884744 | tf_op jit(solution)/shard_map/ppermute | solution.py:238
  30.6 32.0 %collective-permute-start.1 = (bf16[64,2304]{1,0:T(8,128)(2,1)S(1)}, bf16[64,2304]{1,0:T(8,128)(2,1)S(1)}, u32[]{:S(2)}, u32[]{:S(2)}) collective-permute-start(bf16[64,2304]{1,0:T(8,128)(2,1)S(1)} %get-tuple-element.19), channel_id=1, source_target_pairs={{0,129},{1,130},{2,131},{3,128},{4,133},{5,134},{6,135},{7,132},{8... | collective-permute-start | bytes 884744 | tf_op jit(solution)/shard_map/ppermute | solution.py:238
  39.4 73.1 %collective-permute-start.12 = (bf16[256,2304]{1,0:T(8,128)(2,1)S(1)}, bf16[256,2304]{1,0:T(8,128)(2,1)}, u32[]{:S(2)}, u32[]{:S(2)}) collective-permute-start(bf16[256,2304]{1,0:T(8,128)(2,1)S(1)} %get-tuple-element.12), channel_id=1, source_target_pairs={{0,252},{4,0},{8,4},{12,8},{16,12},{20,16},{24,20},{28,24},{32,28}... | collective-permute-start | bytes 3538952 | tf_op jit(solution)/shard_map/ppermute | solution.py:241
  50.8 64.6 %collective-permute-start.11 = (bf16[256,2304]{1,0:T(8,128)(2,1)S(1)}, bf16[256,2304]{1,0:T(8,128)(2,1)}, u32[]{:S(2)}, u32[]{:S(2)}) collective-permute-start(bf16[256,2304]{1,0:T(8,128)(2,1)S(1)} %get-tuple-element.11), channel_id=1, source_target_pairs={{0,252},{4,0},{8,4},{12,8},{16,12},{20,16},{24,20},{28,24},{32,28}... | collective-permute-start | bytes 3538952 | tf_op jit(solution)/shard_map/ppermute | solution.py:241
  51.1 67.2 %collective-permute-start.10 = (bf16[256,2304]{1,0:T(8,128)(2,1)S(1)}, bf16[256,2304]{1,0:T(8,128)(2,1)}, u32[]{:S(2)}, u32[]{:S(2)}) collective-permute-start(bf16[256,2304]{1,0:T(8,128)(2,1)S(1)} %parked_grads.3), channel_id=1, source_target_pairs={{0,252},{4,0},{8,4},{12,8},{16,12},{20,16},{24,20},{28,24},{32,28}... | collective-permute-start | bytes 3538952 | tf_op jit(solution)/shard_map/ppermute | solution.py:241
  68.1 53.1 %collective-permute-start.5 = (bf16[256,2304]{1,0:T(8,128)(2,1)S(1)}, bf16[256,2304]{1,0:T(8,128)(2,1)}, u32[]{:S(2)}, u32[]{:S(2)}) collective-permute-start(bf16[256,2304]{1,0:T(8,128)(2,1)S(1)} %parked_grads.2), channel_id=1, source_target_pairs={{0,252},{4,0},{8,4},{12,8},{16,12},{20,16},{24,20},{28,24},{32,28}... | collective-permute-start | bytes 3538952 | tf_op jit(solution)/shard_map/ppermute | solution.py:241
  69.8 42.7 %collective-permute-start = (s32[1]{0:T(128)}, s32[1]{0:T(128)}, u32[]{:S(2)}, u32[]{:S(2)}) collective-permute-start(s32[1]{0:T(128)} %param.9), channel_id=1, source_target_pairs={{0,252},{4,0},{8,4},{12,8},{16,12},{20,16},{24,20},{28,24},{32,28}... | collective-permute-start | bytes 20 | tf_op jit(solution)/shard_map/ppermute | solution.py:241

commit v2 on v1

v2 whole, which is shorter than its diff:
```python
import functools

import jax
import jax.numpy as jnp
from jax import lax
from jax.experimental import pallas as pl
from jax.experimental.pallas import tpu as pltpu
from jax.sharding import PartitionSpec as P

HD = 128
BLK = 128
KB = 3
HW = 3 * HD
FACTOR = HD**-0.5
FACTOR2 = FACTOR * 1.4426950408889634
KEPT_STEP = 4
PARKED_STEP = 6
VMEM = 56 << 20
HOPS = (3, -3, 1, -1)
KEPT_COST = 1000_000_000
LATE_COST = 4000_000_000
PARKED_COST = 4000_000_000
PARKED_CHUNKS = (6, 6)


def pick(index, values):
    return jnp.where(index == 0, values[0], jnp.where(index == 1, values[1], values[2]))


class Plan:
    def __init__(self, lengths, evicted):
        self.lengths = [lengths[m] for m in range(3)]
        counts = [lax.shift_right_logical(n + (BLK - 1), 7) for n in self.lengths]
        self.starts = [jnp.int32(0), counts[0], counts[0] + counts[1]]
        which = evicted[0]
        self.first = pick(which, self.starts)
        self.span = pick(which, counts)
        self.long = self.span > 1

    def segment(self, block):
        return (block >= self.starts[1]).astype(jnp.int32) + (block >= self.starts[2]).astype(jnp.int32)

    def valid(self, block):
        m = self.segment(block)
        return jnp.clip(pick(m, self.lengths) - BLK * (block - pick(m, self.starts)), 0, BLK)

    def kept(self, slot):
        return jnp.minimum(slot + jnp.where(slot >= self.first, self.span, 0), 3)

    def parked(self, slot):
        return jnp.minimum(self.first + slot, 3)

    def late(self, slot):
        return jnp.where(slot == 0, self.first, jnp.where(self.long, self.parked(1), self.kept(2)))


def nt(a, b):
    return lax.dot_general(a, b, (((1,), (1,)), ((), ())), preferred_element_type=jnp.float32)


def nn(a, b):
    return lax.dot_general(a, b, (((1,), (0,)), ((), ())), preferred_element_type=jnp.float32)


def tn(a, b):
    return lax.dot_general(a, b, (((0,), (0,)), ((), ())), preferred_element_type=jnp.float32)


def attention_grads(q, k, v, grads, valids, joins):
    count = len(q)
    key_ids = lax.broadcasted_iota(jnp.int32, (BLK, BLK), 0)
    query_ids = lax.broadcasted_iota(jnp.int32, (BLK, BLK), 1)
    low = lambda x: x.astype(jnp.bfloat16)
    grads = [jnp.where(key_ids < valids[j], grads[j], jnp.zeros((), jnp.bfloat16)) for j in range(count)]
    both = lambda x, j: jnp.concatenate(x[j : j + 2]) if j + 1 < count else x[j]
    left, right = (lambda x: x[:, :BLK]), (lambda x: x[:, BLK:])

    scores = [nt(k[j], both(q, j)) for j in range(count)]
    prob_grad = [nt(v[j], both(grads, j)) for j in range(count)]
    attend, score_grad = [], []
    for j in range(count):
        here = jnp.where((key_ids <= query_ids) & (key_ids < valids[j]), left(scores[j]) * FACTOR2, -jnp.inf)
        here_grad = left(prob_grad[j])
        top = jnp.max(here, axis=0, keepdims=True)
        if j:
            before = jnp.where(joins[j], right(scores[j - 1]) * FACTOR2, -jnp.inf)
            before_grad = right(prob_grad[j - 1])
            top = jnp.maximum(top, jnp.max(before, axis=0, keepdims=True))
        here = jnp.exp2(here - top)
        total = jnp.sum(here, axis=0, keepdims=True)
        if j:
            before = jnp.exp2(before - top)
            total = total + jnp.sum(before, axis=0, keepdims=True)
        scale = 1.0 / total
        here = here * scale
        row_dot = jnp.sum(here * here_grad, axis=0, keepdims=True)
        if j:
            before = before * scale
            row_dot = row_dot + jnp.sum(before * before_grad, axis=0, keepdims=True)
            attend[j - 1].append(low(before))
            score_grad[j - 1].append(low(before * (before_grad - row_dot)))
        attend.append([low(here)])
        score_grad.append([low(here * (here_grad - row_dot))])
    wide = lambda x: jnp.concatenate(x, axis=1) if len(x) > 1 else x[0]
    dv = [low(nn(wide(attend[j]), both(grads, j))) for j in range(count)]
    dk = [low(nn(wide(score_grad[j]), both(q, j)) * FACTOR) for j in range(count)]
    dq = []
    for j in range(count):
        if j:
            weights, keys = jnp.concatenate([score_grad[j - 1][1], score_grad[j][0]]), jnp.concatenate(k[j - 1 : j + 1])
        else:
            weights, keys = score_grad[0][0], k[0]
        dq.append(low(tn(weights, keys) * FACTOR))
    return dq, dk, dv


def worth(flops):
    return pl.CostEstimate(flops=flops, bytes_accessed=1 << 20, transcendentals=0)


def columns(head, part):
    return slice(head * HW + part * HD, head * HW + (part + 1) * HD)


def kept_kernel(lengths, evicted, rows, g0, g1, g2, early, third):
    plan = Plan(lengths, evicted)
    blocks = [plan.kept(j) for j in range(KB)]
    valids = [plan.valid(b) for b in blocks]
    segments = [plan.segment(b) for b in blocks]
    joins = [None] + [(segments[j] == segments[j - 1]) & jnp.logical_not(plan.long) for j in range(1, KB)]
    for head in range(KEPT_STEP):
        q, k, v = ([rows[j * BLK : (j + 1) * BLK, columns(head, p)] for j in range(KB)] for p in range(3))
        grads = [g[:, head * HD : (head + 1) * HD] for g in (g0, g1, g2)]
        for part, made in enumerate(attention_grads(q, k, v, grads, valids, joins)):
            early[0:BLK, columns(head, part)] = made[0]
            early[BLK : 2 * BLK, columns(head, part)] = made[1]
            third[:, columns(head, part)] = made[2]


def kept_part(lengths, evicted, kept_rows, grad_out, first, heads):
    at = first // KEPT_STEP
    grad_spec = lambda j: pl.BlockSpec(
        (BLK, KEPT_STEP * HD), lambda i, ln, ev: (Plan(ln, ev).kept(j), at + i)
    )
    return pl.pallas_call(
        kept_kernel,
        grid_spec=pltpu.PrefetchScalarGridSpec(
            num_scalar_prefetch=2,
            grid=(heads // KEPT_STEP,),
            in_specs=[pl.BlockSpec((KB * BLK, KEPT_STEP * HW), lambda i, ln, ev: (0, at + i))]
            + [grad_spec(j) for j in range(KB)],
            out_specs=[
                pl.BlockSpec((2 * BLK, KEPT_STEP * HW), lambda i, ln, ev: (0, i)),
                pl.BlockSpec((BLK, KEPT_STEP * HW), lambda i, ln, ev: (0, i)),
            ],
        ),
        out_shape=[
            jax.ShapeDtypeStruct((2 * BLK, heads * HW), jnp.bfloat16),
            jax.ShapeDtypeStruct((BLK, heads * HW), jnp.bfloat16),
        ],
        compiler_params=pltpu.CompilerParams(vmem_limit_bytes=VMEM),
        cost_estimate=worth(heads * KEPT_COST),
        name="kept_grads",
    )(lengths, evicted, kept_rows, grad_out, grad_out, grad_out)


def parked_kernel(lengths, evicted, quarters, r0, r1, r2, r3, g0, g1, third, late, rows):
    plan = Plan(lengths, evicted)
    quarter = BLK // 2
    for d, piece in enumerate((r0, r1, r2, r3)):
        start = pl.multiple_of(quarters[d] * quarter, quarter)
        rows[pl.ds(start, quarter), :] = piece[...]
    valids = [plan.valid(plan.parked(j)) for j in range(2)]
    joins = [None, plan.long]
    for head in range(PARKED_STEP):
        q, k, v = ([rows[j * BLK : (j + 1) * BLK, columns(head, p)] for j in range(2)] for p in range(3))
        grads = [g[:, head * HD : (head + 1) * HD] for g in (g0, g1)]
        grads[1] = jnp.where(plan.long, grads[1], jnp.zeros((), jnp.bfloat16))
        for part, made in enumerate(attention_grads(q, k, v, grads, valids, joins)):
            late[0:BLK, columns(head, part)] = made[0]
            late[BLK : 2 * BLK, columns(head, part)] = jnp.where(
                plan.long, made[1], third[:, columns(head, part)]
            )


def parked_part(lengths, evicted, quarters, pieces, grad_out, third, first, heads, flops):
    at = first // PARKED_STEP
    grad_spec = lambda j: pl.BlockSpec(
        (BLK, PARKED_STEP * HD), lambda i, ln, ev, sh: (Plan(ln, ev).parked(j), at + i)
    )
    return pl.pallas_call(
        parked_kernel,
        grid_spec=pltpu.PrefetchScalarGridSpec(
            num_scalar_prefetch=3,
            grid=(heads // PARKED_STEP,),
            in_specs=[pl.BlockSpec((BLK // 2, PARKED_STEP * HW), lambda i, ln, ev, sh: (0, i))] * 2
            + [pl.BlockSpec((BLK // 2, PARKED_STEP * HW), lambda i, ln, ev, sh: (0, at + i))] * 2
            + [grad_spec(j) for j in range(2)]
            + [pl.BlockSpec((BLK, PARKED_STEP * HW), lambda i, ln, ev, sh: (0, at + i))],
            out_specs=pl.BlockSpec((2 * BLK, PARKED_STEP * HW), lambda i, ln, ev, sh: (0, i)),
            scratch_shapes=[pltpu.VMEM((2 * BLK, PARKED_STEP * HW), jnp.bfloat16)],
        ),
        out_shape=jax.ShapeDtypeStruct((2 * BLK, heads * HW), jnp.bfloat16),
        compiler_params=pltpu.CompilerParams(vmem_limit_bytes=VMEM),
        cost_estimate=worth(heads * flops),
        name="parked_grads",
    )(lengths, evicted, quarters, *pieces, grad_out, grad_out, third)


def place_kernel(slots, firsts, flagged, lengths, evicted, flag, *refs):
    count = len(slots)
    pieces, (out, *rooms), (into, outof) = refs[:count], refs[-count - 3 : -2], refs[-2:]
    plan = Plan(lengths, evicted)

    def copies(n):
        pairs = []
        for slot in range(2):
            rows = pl.ds(slot * BLK, BLK)
            start = pl.multiple_of(slots[n](plan, slot) * BLK, BLK)
            there = out.at[pl.ds(start, BLK), pl.ds(firsts[n] * HW, pieces[n].shape[1])]
            pairs.append(
                (
                    pltpu.make_async_copy(pieces[n].at[rows, :], rooms[n].at[rows, :], into.at[n, slot]),
                    pltpu.make_async_copy(rooms[n].at[rows, :], there, outof.at[n, slot]),
                )
            )
        return pairs

    def move(n):
        pairs = copies(n)
        for fetch, _ in pairs:
            fetch.start()
        for fetch, store in pairs:
            fetch.wait()
            store.start()
        for _, store in pairs:
            store.wait()

    for n in range(count):
        if flagged[n]:
            pl.when(flag[0] > 0)(functools.partial(move, n))
        else:
            move(n)


def place(lengths, evicted, flag, out, total, *items):
    pieces, slots, firsts, flagged = zip(*items)
    base = (lengths, evicted, flag, *pieces) + (() if out is None else (out,))
    smem, hbm = pl.BlockSpec(memory_space=pltpu.SMEM), pl.BlockSpec(memory_space=pltpu.HBM)
    count = len(items)
    return pl.pallas_call(
        functools.partial(place_kernel, slots, firsts, flagged),
        in_specs=[smem] * 3 + [hbm] * (len(base) - 3),
        out_specs=hbm,
        scratch_shapes=[pltpu.VMEM(piece.shape, piece.dtype) for piece in pieces]
        + [pltpu.SemaphoreType.DMA((count, 2)), pltpu.SemaphoreType.DMA((count, 2))],
        out_shape=jax.ShapeDtypeStruct(total, jnp.bfloat16),
        input_output_aliases={} if out is None else {3 + count: 0},
        compiler_params=pltpu.CompilerParams(vmem_limit_bytes=VMEM),
        name="place_rows",
    )(*base)


def shards(kept_rows, parked_rows, grad_out, lengths, evicted):
    sections, peers = lax.axis_size("section"), lax.axis_size("tp")
    half = sections // 2
    ring = 2 * peers
    total = (grad_out.shape[0], kept_rows.shape[1])
    share = total[1]
    spot = 2 * lax.axis_index("tp") + lax.axis_index("section") // half

    def shifted(rows, hops):
        pairs = []
        for s in range(sections):
            for t in range(peers):
                to = (2 * t + s // half + hops) % ring
                pairs.append((s * peers + t, ((s + half) % sections) * peers + to // 2))
        return lax.ppermute(rows, ("section", "tp"), pairs)

    def passed_back(rows, within=sections):
        pairs = [(i, i // within * within + (i - 1) % within) for i in range(sections)]
        return lax.ppermute(rows, "section", pairs)

    def across_ends(rows):
        return lax.ppermute(rows, "section", [(half - 1, sections - 1), (sections - 1, half - 1)])

    next_evicted = passed_back(evicted)
    last = (lax.rem(lax.axis_index("section"), half) == half - 1).astype(jnp.int32).reshape(1)

    def parked_piece(hops, first, heads):
        to = lax.rem(spot + hops + ring, ring) // 2
        rows = lax.dynamic_slice(
            parked_rows, (0, to * share + first * HW), (parked_rows.shape[0], heads * HW)
        )
        return shifted(rows, hops)

    def once(value, *done):
        return lax.optimization_barrier((value, *done))[0]

    quarters = jnp.stack([lax.rem(spot - hops + ring, ring) // 2 for hops in HOPS]).astype(jnp.int32)
    p1, p2 = PARKED_CHUNKS
    far, near = HOPS[:2], HOPS[2:]
    z1 = [parked_piece(hops, 0, p1) for hops in far]
    both = [parked_piece(hops, 0, p1 + p2) for hops in near]
    z2 = [parked_piece(hops, p1, p2) for hops in far]
    early, third = kept_part(lengths, evicted, kept_rows, grad_out, 0, p1 + p2)
    x1 = passed_back(once(early, next_evicted), half)
    late1 = parked_part(lengths, evicted, quarters, z1 + both, grad_out, third, 0, p1, PARKED_COST)
    x2 = passed_back(once(late1, x1))
    late2 = parked_part(once(lengths, late1), evicted, quarters, z2 + both, grad_out, third, p1, p2, LATE_COST)
    x3 = passed_back(late2)
    x1_ends = across_ends(once(x1, late1))
    out = place(lengths, next_evicted, last, None, total, (x1, Plan.kept, 0, False))
    out = place(lengths, next_evicted, last, out, total, (x2, Plan.late, 0, False), (x1_ends, Plan.kept, 0, True))
    return place(lengths, next_evicted, last, out, total, (x3, Plan.late, p1, False))


def solution(mesh):
    in_specs = (
        P("section", "tp"),
        P(("section", "tp"), None),
        P("section", "tp"),
        P(),
        P("section"),
    )
    out_specs = P("section", "tp")
    return jax.shard_map(shards, mesh=mesh, in_specs=in_specs, out_specs=out_specs, check_vma=False)
```

time: 125 us -> 96.2 us (0.77)
  waiting for transfers between devices: 63.7 us -> 37.7 us
  Pallas kernels: 36 us -> 33.2 us
    ppermute x5, waiting for transfers between devices: 42.6 us -> 14.9 us  [the longest x1 10.8 us: across_ends(): lax.ppermute(rows, 'section', [(half - 1, sections - 1), (sections - 1, h...]
    pallas_call x2 -> x1, Pallas kernels: 13.5 us -> 8.45 us  [kept_part(): pl.pallas_call(kept_kernel, grid_spec=pltpu.PrefetchScalarGridSpec(num_sc...]
    pallas_call x4 -> x3, Pallas kernels: 11.5 us -> 13.5 us  [place(): pl.pallas_call(functools.partial(place_kernel, slots, firsts, flagged), i...]
    ppermute x8 -> x6, waiting for transfers between devices: 21 us -> 22.8 us  [shifted(): return lax.ppermute(rows, ('section', 'tp'), pairs)]
    ppermute x8 -> x6, starting transfers between devices: 10.8 us -> 10.4 us  [shifted(): return lax.ppermute(rows, ('section', 'tp'), pairs)]
  transfers between devices with their start and end apart: 13 -> 11, of which waited for: 5 -> 8; matrix products, arithmetic and copies ran while one was open for 0% -> 3% of each run, Pallas kernels for 27% -> 31%
where the time goes in v2:
time: 96.2 us; the launch traced here: 95.8 us
  waiting for transfers between devices  37.7 us (39%)
  Pallas kernels  33.2 us (35%)
  starting transfers between devices  19.6 us (20%)
  local copies, waits for them, and re-layouts  3.81 us (4%)
    ppermute x6, waiting for transfers between devices, shifted(): return lax.ppermute(rows, ('section', 'tp'), pairs)  22.8 us
    pallas_call x3, Pallas kernels, place(): pl.pallas_call(functools.partial(place_kernel, slots, firsts, flagged), i...  13.5 us
    pallas_call x2, Pallas kernels, parked_part(): pl.pallas_call(parked_kernel, grid_spec=pltpu.PrefetchScalarGridSpec(num_...  11.2 us
    ppermute x1, waiting for transfers between devices, across_ends(): lax.ppermute(rows, 'section', [(half - 1, sections - 1), (sections - 1, h...  10.8 us
    ppermute x6, starting transfers between devices, shifted(): return lax.ppermute(rows, ('section', 'tp'), pairs)  10.4 us
    pallas_call x1, Pallas kernels, kept_part(): pl.pallas_call(kept_kernel, grid_spec=pltpu.PrefetchScalarGridSpec(num_sc...  8.45 us
    ppermute x1, starting transfers between devices, across_ends(): lax.ppermute(rows, 'section', [(half - 1, sections - 1), (sections - 1, h...  4.87 us
    ppermute x4, starting transfers between devices, passed_back(): return lax.ppermute(rows, 'section', pairs)  4.31 us
  transfers between devices with their start and end apart: 11, of which 8 were waited for; matrix products, arithmetic and copies ran while one was open for 3% of the time, Pallas kernels for 31%

profile of v2, /device:TPU:63, one launch (start us, length us, event | category | flops | bytes accessed | tf_op | source)
XLA Modules:
  0.0 95.8 jit_solution(11430749044905865139)
XLA Ops:
  0.7 2.1 %constant_dynamic-slice_fusion = (bf16[64,2304]{1,0:T(8,128)(2,1)}, bf16[64,2304]{1,0:T(8,128)(2,1)S(1)}, bf16[64,2304]{1,0:T(8,128)(2,1)S(1)}, bf16[64,2304]{1,0:T(8,128)(2,1)}) fusion(bf16[64,18432]{1,0:T(8,128)(2,1)} %param.6, s32[]{:T(128)S(6)} %select_n.51, s32[]{:T(128)S(6)} %select_n.47, s32[]{:T(128)S(6)} %select_n.46, s32[]{:T(128)S(6)} %select_n.50), kind=kLoop, calls=%fused_computation | loop fusion | bytes 2359312 | tf_op jit(solution)/shard_map/dynamic_slice | solution.py:292
  2.8 5.6 %collective-permute-start.2 = (bf16[64,2304]{1,0:T(8,128)(2,1)S(1)}, bf16[64,2304]{1,0:T(8,128)(2,1)S(1)}, u32[]{:S(2)}, u32[]{:S(2)}) collective-permute-start(bf16[64,2304]{1,0:T(8,128)(2,1)S(1)} %get-tuple-element.18), channel_id=1, source_target_pairs={{0,130},{1,131},{2,128},{3,129},{4,134},{5,135},{6,132},{7,133},{8... | collective-permute-start | bytes 884744 | tf_op jit(solution)/shard_map/ppermute | solution.py:278
  8.5 0.8 collective-permute-start.4
  9.3 0.7 collective-permute-start.3
  10.7 8.5 %kept_grads.1 = (bf16[256,4608]{1,0:T(8,128)(2,1)}, bf16[128,4608]{1,0:T(8,128)(2,1)}) custom-call(s32[3]{0:T(128)} %lengths.10, s32[1]{0:T(128)S(6)} %copy.10.evicted, bf16[384,4608]{1,0:T(8,128)(2,1)} %rows.1, bf16[512,1536]{1,0:T(8,128)(2,1)} %g1.5, bf16[512,1536]{1,0:T(8,128)(2,1)} %g1.5, bf16[512,1536]{1,0:T(8,128)(2,1)} %g1.5), custom_call_target="tpu_custom_call" | custom-call | flops 12000000000 | bytes 1048576 | tf_op jit(solution)/shard_map/kept_grads/pallas_call | solution.py:145
  19.1 1.3 %collective-permute-start.8 = (bf16[256,4608]{1,0:T(8,128)(2,1)}, bf16[256,4608]{1,0:T(8,128)(2,1)S(1)}, u32[]{:S(2)}, u32[]{:S(2)}) collective-permute-start(bf16[256,4608]{1,0:T(8,128)(2,1)} %get-tuple-element.14), channel_id=1, source_target_pairs={{0,124},{4,0},{8,4},{12,8},{16,12},{20,16},{24,20},{28,24},{32,28}... | collective-permute-start | bytes 7077896 | tf_op jit(solution)/shard_map/ppermute | solution.py:282
  21.0 5.3 %collective-permute-done.2.r1 = bf16[64,2304]{1,0:T(8,128)(2,1)S(1)} collective-permute-done((bf16[64,2304]{1,0:T(8,128)(2,1)S(1)}, bf16[64,2304]{1,0:T(8,128)(2,1)S(1)}, u32[]{:S(2)}, u32[]{:S(2)}) %collective-permute-start.2) | collective-permute-done | bytes 294944 | tf_op jit(solution)/shard_map/ppermute | solution.py:278
  26.3 3.3 %collective-permute-start.6 = (bf16[64,2304]{1,0:T(8,128)(2,1)}, bf16[64,2304]{1,0:T(8,128)(2,1)S(1)}, u32[]{:S(2)}, u32[]{:S(2)}) collective-permute-start(bf16[64,2304]{1,0:T(8,128)(2,1)} %get-tuple-element.17), channel_id=1, source_target_pairs={{0,130},{1,131},{2,128},{3,129},{4,134},{5,135},{6,132},{7,133},{8... | collective-permute-start | bytes 884744 | tf_op jit(solution)/shard_map/ppermute | solution.py:278
  29.6 1.8 %collective-permute-done.1.r0 = bf16[64,2304]{1,0:T(8,128)(2,1)S(1)} collective-permute-done((bf16[64,2304]{1,0:T(8,128)(2,1)S(1)}, bf16[64,2304]{1,0:T(8,128)(2,1)S(1)}, u32[]{:S(2)}, u32[]{:S(2)}) %collective-permute-start.1) | collective-permute-done | bytes 294944 | tf_op jit(solution)/shard_map/ppermute | solution.py:278
  31.5 6.8 %collective-permute-done.4.r3 = bf16[64,4608]{1,0:T(8,128)(2,1)S(1)} collective-permute-done((bf16[64,4608]{1,0:T(8,128)(2,1)S(1)}, bf16[64,4608]{1,0:T(8,128)(2,1)S(1)}, u32[]{:S(2)}, u32[]{:S(2)}) %collective-permute-start.4) | collective-permute-done | bytes 589856 | tf_op jit(solution)/shard_map/ppermute | solution.py:278
  38.3 2.9 %collective-permute-done.3.r2 = bf16[64,4608]{1,0:T(8,128)(2,1)S(1)} collective-permute-done((bf16[64,4608]{1,0:T(8,128)(2,1)S(1)}, bf16[64,4608]{1,0:T(8,128)(2,1)S(1)}, u32[]{:S(2)}, u32[]{:S(2)}) %collective-permute-start.3) | collective-permute-done | bytes 589856 | tf_op jit(solution)/shard_map/ppermute | solution.py:278
  41.3 0.8 copy-done.4
  42.1 5.6 %parked_grads.2 = bf16[256,2304]{1,0:T(8,128)(2,1)} custom-call(s32[3]{0:T(128)} %lengths.10, s32[1]{0:T(128)S(6)} %copy.10.evicted, s32[4]{0:T(128)} %pad_add_fusion.quarters, bf16[64,2304]{1,0:T(8,128)(2,1)} %copy-done.6, bf16[64,2304]{1,0:T(8,128)(2,1)} %copy-done.5, bf16[64,4608]{1,0:T(8,128)(2,1)} %copy-done.4, bf16[64,4608]{1,0:T(8,128)(2,1)} %copy-done.3, ...), custom_call_target="tpu_custom_call" | custom-call | flops 24000000000 | bytes 1048576 | tf_op jit(solution)/shard_map/parked_grads/pallas_call | solution.py:191
  47.7 4.1 %collective-permute-done.8.refs_0_ = bf16[256,4608]{1,0:T(8,128)(2,1)S(1)} collective-permute-done((bf16[256,4608]{1,0:T(8,128)(2,1)}, bf16[256,4608]{1,0:T(8,128)(2,1)S(1)}, u32[]{:S(2)}, u32[]{:S(2)}) %collective-permute-start.8) | collective-permute-done | bytes 2359328 | tf_op jit(solution)/shard_map/ppermute | solution.py:282
  51.8 4.9 %collective-permute-start.10 = (bf16[256,4608]{1,0:T(8,128)(2,1)S(1)}, bf16[256,4608]{1,0:T(8,128)(2,1)}, u32[]{:S(2)}, u32[]{:S(2)}) collective-permute-start(bf16[256,4608]{1,0:T(8,128)(2,1)S(1)} %collective-permute-done.8.refs_0_), channel_id=1, source_target_pairs={{124,252},{252,124},{125,253},{253,125},{126,254},{254,126},{127,2... | collective-permute-start | bytes 7077896 | tf_op jit(solution)/shard_map/ppermute | solution.py:285
  56.7 1.3 %collective-permute-done.6.r1 = bf16[64,2304]{1,0:T(8,128)(2,1)S(1)} collective-permute-done((bf16[64,2304]{1,0:T(8,128)(2,1)}, bf16[64,2304]{1,0:T(8,128)(2,1)S(1)}, u32[]{:S(2)}, u32[]{:S(2)}) %collective-permute-start.6) | collective-permute-done | bytes 294944 | tf_op jit(solution)/shard_map/ppermute | solution.py:278
  58.0 4.6 %collective-permute-done.5.r0 = bf16[64,2304]{1,0:T(8,128)(2,1)S(1)} collective-permute-done((bf16[64,2304]{1,0:T(8,128)(2,1)}, bf16[64,2304]{1,0:T(8,128)(2,1)S(1)}, u32[]{:S(2)}, u32[]{:S(2)}) %collective-permute-start.5) | collective-permute-done | bytes 294944 | tf_op jit(solution)/shard_map/ppermute | solution.py:278
  62.6 0.7 copy-done.8
  63.3 5.6 %parked_grads.3 = bf16[256,2304]{1,0:T(8,128)(2,1)} custom-call(s32[3]{0:T(128)} %lengths.10, s32[1]{0:T(128)S(6)} %copy.10.evicted, s32[4]{0:T(128)} %pad_add_fusion.quarters, bf16[64,2304]{1,0:T(8,128)(2,1)} %copy-done.8, bf16[64,2304]{1,0:T(8,128)(2,1)} %copy-done.7, bf16[64,4608]{1,0:T(8,128)(2,1)} %copy-done.4, bf16[64,4608]{1,0:T(8,128)(2,1)} %copy-done.3, ...), custom_call_target="tpu_custom_call" | custom-call | flops 24000000000 | bytes 1048576 | tf_op jit(solution)/shard_map/parked_grads/pallas_call | solution.py:191
  68.9 2.3 %collective-permute-start.7 = (bf16[256,2304]{1,0:T(8,128)(2,1)}, bf16[256,2304]{1,0:T(8,128)(2,1)}, u32[]{:S(2)}, u32[]{:S(2)}) collective-permute-start(bf16[256,2304]{1,0:T(8,128)(2,1)} %parked_grads.3), channel_id=1, source_target_pairs={{0,252},{4,0},{8,4},{12,8},{16,12},{20,16},{24,20},{28,24},{32,28}... | collective-permute-start | bytes 3538952 | tf_op jit(solution)/shard_map/ppermute | solution.py:282
  71.3 4.0 %place_rows.3.refs_2_ = bf16[512,4608]{1,0:T(8,128)(2,1)} custom-call(s32[3]{0:T(128)} %lengths.10, s32[1]{0:T(128)} %collective-permute-done.evicted, s32[1]{0:T(128)} %bitcast.flag, bf16[256,4608]{1,0:T(8,128)(2,1)} %copy-done.1), custom_call_target="tpu_custom_call" | custom-call | tf_op jit(solution)/shard_map/place_rows/pallas_call | solution.py:251
  75.3 10.8 %collective-permute-done.10.refs_1_ = bf16[256,4608]{1,0:T(8,128)(2,1)} collective-permute-done((bf16[256,4608]{1,0:T(8,128)(2,1)S(1)}, bf16[256,4608]{1,0:T(8,128)(2,1)}, u32[]{:S(2)}, u32[]{:S(2)}) %collective-permute-start.10) | collective-permute-done | bytes 2359328 | tf_op jit(solution)/shard_map/ppermute | solution.py:285
  86.1 6.1 %place_rows.4.refs_1_ = bf16[512,4608]{1,0:T(8,128)(2,1)} custom-call(s32[3]{0:T(128)} %lengths.10, s32[1]{0:T(128)} %collective-permute-done.evicted, s32[1]{0:T(128)} %bitcast.flag, bf16[256,2304]{1,0:T(8,128)(2,1)} %copy-done.2, bf16[256,4608]{1,0:T(8,128)(2,1)} %collective-permute-done.10.refs_1_, ...), custom_call_target="tpu_custom_call", output_to_operand_aliasing={{}: (5, {})} | custom-call | tf_op jit(solution)/shard_map/place_rows/pallas_call | solution.py:251
  92.3 3.4 %place_rows.5 = bf16[512,4608]{1,0:T(8,128)(2,1)} custom-call(s32[3]{0:T(128)} %lengths.10, s32[1]{0:T(128)} %collective-permute-done.evicted, s32[1]{0:T(128)} %bitcast.flag, bf16[256,2304]{1,0:T(8,128)(2,1)} %collective-permute-done.7.refs_0_, bf16[512,4608]{1,0:T(8,128)(2,1)} %place_rows.4.refs_1_), custom_call_target="tpu_custom_call", output_to_operand_aliasing={{}: (4, {})} | custom-call | tf_op jit(solution)/shard_map/place_rows/pallas_call | solution.py:251
  (25 shorter events, 1.4 us)
Async XLA Ops:
  0.0 8.4 %copy-start = (bf16[64,18432]{1,0:T(8,128)(2,1)S(1)}, bf16[64,18432]{1,0:T(8,128)(2,1)}, u32[]{:S(2)}) copy-start(bf16[64,18432]{1,0:T(8,128)(2,1)} %param.6) | copy-start | bytes 7077892
  0.0 19.1 %collective-permute-start = (s32[1]{0:T(128)}, s32[1]{0:T(128)}, u32[]{:S(2)}, u32[]{:S(2)}) collective-permute-start(s32[1]{0:T(128)} %param.9), channel_id=1, source_target_pairs={{0,252},{4,0},{8,4},{12,8},{16,12},{20,16},{24,20},{28,24},{32,28}... | collective-permute-start | bytes 20 | tf_op jit(solution)/shard_map/ppermute | solution.py:282
  2.8 23.5 %collective-permute-start.2 = (bf16[64,2304]{1,0:T(8,128)(2,1)S(1)}, bf16[64,2304]{1,0:T(8,128)(2,1)S(1)}, u32[]{:S(2)}, u32[]{:S(2)}) collective-permute-start(bf16[64,2304]{1,0:T(8,128)(2,1)S(1)} %get-tuple-element.18), channel_id=1, source_target_pairs={{0,130},{1,131},{2,128},{3,129},{4,134},{5,135},{6,132},{7,133},{8... | collective-permute-start | bytes 884744 | tf_op jit(solution)/shard_map/ppermute | solution.py:278
  8.4 23.1 %collective-permute-start.1 = (bf16[64,2304]{1,0:T(8,128)(2,1)S(1)}, bf16[64,2304]{1,0:T(8,128)(2,1)S(1)}, u32[]{:S(2)}, u32[]{:S(2)}) collective-permute-start(bf16[64,2304]{1,0:T(8,128)(2,1)S(1)} %get-tuple-element.19), channel_id=1, source_target_pairs={{0,129},{1,130},{2,131},{3,128},{4,133},{5,134},{6,135},{7,132},{8... | collective-permute-start | bytes 884744 | tf_op jit(solution)/shard_map/ppermute | solution.py:278
  8.5 29.8 %collective-permute-start.4 = (bf16[64,4608]{1,0:T(8,128)(2,1)S(1)}, bf16[64,4608]{1,0:T(8,128)(2,1)S(1)}, u32[]{:S(2)}, u32[]{:S(2)}) collective-permute-start(bf16[64,4608]{1,0:T(8,128)(2,1)S(1)} %get-tuple-element.21), channel_id=1, source_target_pairs={{0,131},{1,128},{2,129},{3,130},{4,135},{5,132},{6,133},{7,134},{8... | collective-permute-start | bytes 1769480 | tf_op jit(solution)/shard_map/ppermute | solution.py:278
  9.3 32.0 %collective-permute-start.3 = (bf16[64,4608]{1,0:T(8,128)(2,1)S(1)}, bf16[64,4608]{1,0:T(8,128)(2,1)S(1)}, u32[]{:S(2)}, u32[]{:S(2)}) collective-permute-start(bf16[64,4608]{1,0:T(8,128)(2,1)S(1)} %get-tuple-element.22), channel_id=1, source_target_pairs={{0,128},{1,129},{2,130},{3,131},{4,132},{5,133},{6,134},{7,135},{8... | collective-permute-start | bytes 1769480 | tf_op jit(solution)/shard_map/ppermute | solution.py:278
  19.1 32.7 %collective-permute-start.8 = (bf16[256,4608]{1,0:T(8,128)(2,1)}, bf16[256,4608]{1,0:T(8,128)(2,1)S(1)}, u32[]{:S(2)}, u32[]{:S(2)}) collective-permute-start(bf16[256,4608]{1,0:T(8,128)(2,1)} %get-tuple-element.14), channel_id=1, source_target_pairs={{0,124},{4,0},{8,4},{12,8},{16,12},{20,16},{24,20},{28,24},{32,28}... | collective-permute-start | bytes 7077896 | tf_op jit(solution)/shard_map/ppermute | solution.py:282
  26.3 14.9 %copy-start.5 = (bf16[64,2304]{1,0:T(8,128)(2,1)}, bf16[64,2304]{1,0:T(8,128)(2,1)S(1)}, u32[]{:S(2)}) copy-start(bf16[64,2304]{1,0:T(8,128)(2,1)S(1)} %collective-permute-done.2.r1) | copy-start | bytes 884740
  26.3 31.7 %collective-permute-start.6 = (bf16[64,2304]{1,0:T(8,128)(2,1)}, bf16[64,2304]{1,0:T(8,128)(2,1)S(1)}, u32[]{:S(2)}, u32[]{:S(2)}) collective-permute-start(bf16[64,2304]{1,0:T(8,128)(2,1)} %get-tuple-element.17), channel_id=1, source_target_pairs={{0,130},{1,131},{2,128},{3,129},{4,134},{5,135},{6,132},{7,133},{8... | collective-permute-start | bytes 884744 | tf_op jit(solution)/shard_map/ppermute | solution.py:278
  31.5 9.8 %copy-start.6 = (bf16[64,2304]{1,0:T(8,128)(2,1)}, bf16[64,2304]{1,0:T(8,128)(2,1)S(1)}, u32[]{:S(2)}) copy-start(bf16[64,2304]{1,0:T(8,128)(2,1)S(1)} %collective-permute-done.1.r0) | copy-start | bytes 884740
  31.5 31.2 %collective-permute-start.5 = (bf16[64,2304]{1,0:T(8,128)(2,1)}, bf16[64,2304]{1,0:T(8,128)(2,1)S(1)}, u32[]{:S(2)}, u32[]{:S(2)}) collective-permute-start(bf16[64,2304]{1,0:T(8,128)(2,1)} %get-tuple-element.20), channel_id=1, source_target_pairs={{0,129},{1,130},{2,131},{3,128},{4,133},{5,134},{6,135},{7,132},{8... | collective-permute-start | bytes 884744 | tf_op jit(solution)/shard_map/ppermute | solution.py:278
  38.3 3.0 %copy-start.3 = (bf16[64,4608]{1,0:T(8,128)(2,1)}, bf16[64,4608]{1,0:T(8,128)(2,1)S(1)}, u32[]{:S(2)}) copy-start(bf16[64,4608]{1,0:T(8,128)(2,1)S(1)} %collective-permute-done.4.r3) | copy-start | bytes 1769476
  41.2 0.9 copy-start.4
  51.8 17.1 %copy-start.1 = (bf16[256,4608]{1,0:T(8,128)(2,1)}, bf16[256,4608]{1,0:T(8,128)(2,1)S(1)}, u32[]{:S(2)}) copy-start(bf16[256,4608]{1,0:T(8,128)(2,1)S(1)} %collective-permute-done.8.refs_0_) | copy-start | bytes 7077892
  51.8 23.5 %collective-permute-start.9 = (bf16[256,2304]{1,0:T(8,128)(2,1)}, bf16[256,2304]{1,0:T(8,128)(2,1)S(1)}, u32[]{:S(2)}, u32[]{:S(2)}) collective-permute-start(bf16[256,2304]{1,0:T(8,128)(2,1)} %parked_grads.2), channel_id=1, source_target_pairs={{0,252},{4,0},{8,4},{12,8},{16,12},{20,16},{24,20},{28,24},{32,28}... | collective-permute-start | bytes 3538952 | tf_op jit(solution)/shard_map/ppermute | solution.py:282
  51.8 34.3 %collective-permute-start.10 = (bf16[256,4608]{1,0:T(8,128)(2,1)S(1)}, bf16[256,4608]{1,0:T(8,128)(2,1)}, u32[]{:S(2)}, u32[]{:S(2)}) collective-permute-start(bf16[256,4608]{1,0:T(8,128)(2,1)S(1)} %collective-permute-done.8.refs_0_), channel_id=1, source_target_pairs={{124,252},{252,124},{125,253},{253,125},{126,254},{254,126},{127,2... | collective-permute-start | bytes 7077896 | tf_op jit(solution)/shard_map/ppermute | solution.py:285
  58.0 4.6 %copy-start.7 = (bf16[64,2304]{1,0:T(8,128)(2,1)}, bf16[64,2304]{1,0:T(8,128)(2,1)S(1)}, u32[]{:S(2)}) copy-start(bf16[64,2304]{1,0:T(8,128)(2,1)S(1)} %collective-permute-done.6.r1) | copy-start | bytes 884740
  62.6 0.7 copy-start.8
  68.9 23.3 %collective-permute-start.7 = (bf16[256,2304]{1,0:T(8,128)(2,1)}, bf16[256,2304]{1,0:T(8,128)(2,1)}, u32[]{:S(2)}, u32[]{:S(2)}) collective-permute-start(bf16[256,2304]{1,0:T(8,128)(2,1)} %parked_grads.3), channel_id=1, source_target_pairs={{0,252},{4,0},{8,4},{12,8},{16,12},{20,16},{24,20},{28,24},{32,28}... | collective-permute-start | bytes 3538952 | tf_op jit(solution)/shard_map/ppermute | solution.py:282
  75.3 10.8 %copy-start.2 = (bf16[256,2304]{1,0:T(8,128)(2,1)}, bf16[256,2304]{1,0:T(8,128)(2,1)S(1)}, u32[]{:S(2)}) copy-start(bf16[256,2304]{1,0:T(8,128)(2,1)S(1)} %collective-permute-done.9.refs_0_) | copy-start | bytes 3538948

commit v3 on v2

--- a/solution.py
+++ b/solution.py
@@ -15,12 +15,14 @@
 FACTOR2 = FACTOR * 1.4426950408889634
 KEPT_STEP = 4
 PARKED_STEP = 6
-VMEM = 56 << 20
+VMEM = 20 << 20
 HOPS = (3, -3, 1, -1)
 KEPT_COST = 1000_000_000
-LATE_COST = 4000_000_000
+LATE_COSTS = (8000_000_000,)
+PLACE_COST = 1000_000_000
 PARKED_COST = 4000_000_000
 PARKED_CHUNKS = (6, 6)
+LAST_CHUNKS = (6,)
 
 
 def pick(index, values):
@@ -118,6 +120,10 @@
     return pl.CostEstimate(flops=flops, bytes_accessed=1 << 20, transcendentals=0)
 
 
+def in_hbm(x):
+    return pltpu.with_memory_space_constraint(x, pltpu.HBM)
+
+
 def columns(head, part):
     return slice(head * HW + part * HD, head * HW + (part + 1) * HD)
 
@@ -161,18 +167,20 @@
         compiler_params=pltpu.CompilerParams(vmem_limit_bytes=VMEM),
         cost_estimate=worth(heads * KEPT_COST),
         name="kept_grads",
-    )(lengths, evicted, kept_rows, grad_out, grad_out, grad_out)
-
-
-def parked_kernel(lengths, evicted, quarters, r0, r1, r2, r3, g0, g1, third, late, rows):
+    )(lengths, evicted, in_hbm(kept_rows), *[in_hbm(grad_out)] * 3)
+
+
+def parked_kernel(ats, lengths, evicted, quarters, r0, r1, r2, r3, g0, g1, third, late, rows):
     plan = Plan(lengths, evicted)
     quarter = BLK // 2
     for d, piece in enumerate((r0, r1, r2, r3)):
         start = pl.multiple_of(quarters[d] * quarter, quarter)
-        rows[pl.ds(start, quarter), :] = piece[...]
+        width = rows.shape[1]
+        first = pl.multiple_of((ats[d] + pl.program_id(0)) * width, BLK)
+        rows[pl.ds(start, quarter), :] = piece[:, pl.ds(first, width)]
     valids = [plan.valid(plan.parked(j)) for j in range(2)]
     joins = [None, plan.long]
-    for head in range(PARKED_STEP):
+    for head in range(rows.shape[1] // HW):
         q, k, v = ([rows[j * BLK : (j + 1) * BLK, columns(head, p)] for j in range(2)] for p in range(3))
         grads = [g[:, head * HD : (head + 1) * HD] for g in (g0, g1)]
         grads[1] = jnp.where(plan.long, grads[1], jnp.zeros((), jnp.bfloat16))
@@ -183,80 +191,74 @@
             )
 
 
-def parked_part(lengths, evicted, quarters, pieces, grad_out, third, first, heads, flops):
-    at = first // PARKED_STEP
+def parked_part(lengths, evicted, quarters, pieces, grad_out, third, first, heads, flops, far_first=0):
+    step = min(PARKED_STEP, heads)
+    at, far_at = first // step, (first - far_first) // step
     grad_spec = lambda j: pl.BlockSpec(
-        (BLK, PARKED_STEP * HD), lambda i, ln, ev, sh: (Plan(ln, ev).parked(j), at + i)
+        (BLK, step * HD), lambda i, ln, ev, sh: (Plan(ln, ev).parked(j), at + i)
     )
     return pl.pallas_call(
-        parked_kernel,
+        functools.partial(parked_kernel, (far_at, far_at, at, at)),
         grid_spec=pltpu.PrefetchScalarGridSpec(
             num_scalar_prefetch=3,
-            grid=(heads // PARKED_STEP,),
-            in_specs=[pl.BlockSpec((BLK // 2, PARKED_STEP * HW), lambda i, ln, ev, sh: (0, i))] * 2
-            + [pl.BlockSpec((BLK // 2, PARKED_STEP * HW), lambda i, ln, ev, sh: (0, at + i))] * 2
+            grid=(heads // step,),
+            in_specs=[pl.BlockSpec(memory_space=pltpu.VMEM)] * 4
             + [grad_spec(j) for j in range(2)]
-            + [pl.BlockSpec((BLK, PARKED_STEP * HW), lambda i, ln, ev, sh: (0, at + i))],
-            out_specs=pl.BlockSpec((2 * BLK, PARKED_STEP * HW), lambda i, ln, ev, sh: (0, i)),
-            scratch_shapes=[pltpu.VMEM((2 * BLK, PARKED_STEP * HW), jnp.bfloat16)],
+            + [pl.BlockSpec((BLK, step * HW), lambda i, ln, ev, sh: (0, at + i))],
+            out_specs=pl.BlockSpec((2 * BLK, step * HW), lambda i, ln, ev, sh: (0, i)),
+            scratch_shapes=[pltpu.VMEM((2 * BLK, step * HW), jnp.bfloat16)],
         ),
         out_shape=jax.ShapeDtypeStruct((2 * BLK, heads * HW), jnp.bfloat16),
         compiler_params=pltpu.CompilerParams(vmem_limit_bytes=VMEM),
         cost_estimate=worth(heads * flops),
         name="parked_grads",
-    )(lengths, evicted, quarters, *pieces, grad_out, grad_out, third)
+    )(lengths, evicted, quarters, *pieces, *[in_hbm(grad_out)] * 2, in_hbm(third))
 
 
 def place_kernel(slots, firsts, flagged, lengths, evicted, flag, *refs):
     count = len(slots)
-    pieces, (out, *rooms), (into, outof) = refs[:count], refs[-count - 3 : -2], refs[-2:]
+    pieces, (out, sems) = refs[:count], refs[-2:]
     plan = Plan(lengths, evicted)
 
-    def copies(n):
-        pairs = []
+    def store(n, slot):
+        start = pl.multiple_of(slots[n](plan, slot) * BLK, BLK)
+        return pltpu.make_async_copy(
+            pieces[n].at[pl.ds(slot * BLK, BLK), :],
+            out.at[pl.ds(start, BLK), pl.ds(firsts[n] * HW, pieces[n].shape[1])],
+            sems.at[n, slot],
+        )
+
+    def begin(n):
         for slot in range(2):
-            rows = pl.ds(slot * BLK, BLK)
-            start = pl.multiple_of(slots[n](plan, slot) * BLK, BLK)
-            there = out.at[pl.ds(start, BLK), pl.ds(firsts[n] * HW, pieces[n].shape[1])]
-            pairs.append(
-                (
-                    pltpu.make_async_copy(pieces[n].at[rows, :], rooms[n].at[rows, :], into.at[n, slot]),
-                    pltpu.make_async_copy(rooms[n].at[rows, :], there, outof.at[n, slot]),
-                )
-            )
-        return pairs
-
-    def move(n):
-        pairs = copies(n)
-        for fetch, _ in pairs:
-            fetch.start()
-        for fetch, store in pairs:
-            fetch.wait()
-            store.start()
-        for _, store in pairs:
-            store.wait()
-
-    for n in range(count):
-        if flagged[n]:
-            pl.when(flag[0] > 0)(functools.partial(move, n))
-        else:
-            move(n)
+            store(n, slot).start()
+
+    def finish(n):
+        for slot in range(2):
+            store(n, slot).wait()
+
+    for step in (begin, finish):
+        for n in range(count):
+            run = functools.partial(step, n)
+            if flagged[n]:
+                pl.when(flag[0] > 0)(run)
+            else:
+                run()
 
 
 def place(lengths, evicted, flag, out, total, *items):
     pieces, slots, firsts, flagged = zip(*items)
     base = (lengths, evicted, flag, *pieces) + (() if out is None else (out,))
-    smem, hbm = pl.BlockSpec(memory_space=pltpu.SMEM), pl.BlockSpec(memory_space=pltpu.HBM)
+    smem, free = pl.BlockSpec(memory_space=pltpu.SMEM), pl.BlockSpec(memory_space=pl.ANY)
     count = len(items)
     return pl.pallas_call(
         functools.partial(place_kernel, slots, firsts, flagged),
-        in_specs=[smem] * 3 + [hbm] * (len(base) - 3),
-        out_specs=hbm,
-        scratch_shapes=[pltpu.VMEM(piece.shape, piece.dtype) for piece in pieces]
-        + [pltpu.SemaphoreType.DMA((count, 2)), pltpu.SemaphoreType.DMA((count, 2))],
+        in_specs=[smem] * 3 + [free] * (len(base) - 3),
+        out_specs=free,
+        scratch_shapes=[pltpu.SemaphoreType.DMA((count, 2))],
         out_shape=jax.ShapeDtypeStruct(total, jnp.bfloat16),
         input_output_aliases={} if out is None else {3 + count: 0},
-        compiler_params=pltpu.CompilerParams(vmem_limit_bytes=VMEM),
+        compiler_params=pltpu.CompilerParams(vmem_limit_bytes=1 << 20),
+        cost_estimate=worth(PLACE_COST),
         name="place_rows",
     )(*base)
 
@@ -307,12 +309,18 @@
     x1 = passed_back(once(early, next_evicted), half)
     late1 = parked_part(lengths, evicted, quarters, z1 + both, grad_out, third, 0, p1, PARKED_COST)
     x2 = passed_back(once(late1, x1))
-    late2 = parked_part(once(lengths, late1), evicted, quarters, z2 + both, grad_out, third, p1, p2, LATE_COST)
-    x3 = passed_back(late2)
     x1_ends = across_ends(once(x1, late1))
     out = place(lengths, next_evicted, last, None, total, (x1, Plan.kept, 0, False))
-    out = place(lengths, next_evicted, last, out, total, (x2, Plan.late, 0, False), (x1_ends, Plan.kept, 0, True))
-    return place(lengths, next_evicted, last, out, total, (x3, Plan.late, p1, False))
+    pieces = []
+    before, first = (late1, out), p1
+    for heads, flops in zip(LAST_CHUNKS, LATE_COSTS):
+        late = parked_part(
+            once(lengths, *before), evicted, quarters, z2 + both, grad_out, third, first, heads, flops, p1
+        )
+        pieces.append((passed_back(late), Plan.late, first, False))
+        before, first = (late, x2), first + heads
+    out = place(lengths, next_evicted, last, out, total, (x2, Plan.late, 0, False))
+    return place(lengths, next_evicted, last, out, total, (x1_ends, Plan.kept, 0, True), *pieces)
 
 
 def solution(mesh):

time: 96.2 us -> 92.4 us (0.960); the launches traced: 95.8 us -> 90.8 us
  Pallas kernels: 33.2 us -> 23.7 us
  waiting for transfers between devices: 37.7 us -> 43.6 us
  starting transfers between devices: 19.6 us -> 18.1 us
    ppermute x4, waiting for transfers between devices: 4.07 us -> 24.1 us  [passed_back(): return lax.ppermute(rows, 'section', pairs)]
    ppermute x1, waiting for transfers between devices: 10.8 us -> 0.01 us  [across_ends(): lax.ppermute(rows, 'section', [(half - 1, sections - 1), (sections - 1, h...]
    pallas_call x3, Pallas kernels: 13.5 us -> 7.76 us  [place(): pl.pallas_call(functools.partial(place_kernel, slots, firsts, flagged), i...]
    ppermute x6, waiting for transfers between devices: 22.8 us -> 19.4 us  [shifted(): return lax.ppermute(rows, ('section', 'tp'), pairs)]
    pallas_call x2, Pallas kernels: 11.2 us -> 8.38 us  [parked_part(): pl.pallas_call(functools.partial(parked_kernel, (far_at, far_at, at, at))...]
    ppermute x4, starting transfers between devices: 4.31 us -> 2.86 us  [passed_back(): return lax.ppermute(rows, 'section', pairs)]
    dynamic_slice x2, local copies, waits for them, and re-layouts: 2.22 us -> 3.44 us  [parked_piece(): lax.dynamic_slice(parked_rows, (0, to * share + first * HW), (parked_rows...]
  transfers between devices with their start and end apart: 11 -> 11, of which waited for: 8 -> 8; matrix products, arithmetic and copies ran while one was open for 3% -> 4% of each run, Pallas kernels for 31% -> 23%
where the time goes in v3:
time: 92.4 us; the launch traced here: 90.8 us
  waiting for transfers between devices  43.6 us (47%)
  Pallas kernels  23.7 us (26%)
  starting transfers between devices  18.1 us (20%)
  local copies, waits for them, and re-layouts  4.47 us (5%)
    ppermute x4, waiting for transfers between devices, passed_back(): return lax.ppermute(rows, 'section', pairs)  24.1 us
    ppermute x6, waiting for transfers between devices, shifted(): return lax.ppermute(rows, ('section', 'tp'), pairs)  19.4 us
    ppermute x6, starting transfers between devices, shifted(): return lax.ppermute(rows, ('section', 'tp'), pairs)  10.4 us
    pallas_call x2, Pallas kernels, parked_part(): pl.pallas_call(functools.partial(parked_kernel, (far_at, far_at, at, at))...  8.38 us
    pallas_call x3, Pallas kernels, place(): pl.pallas_call(functools.partial(place_kernel, slots, firsts, flagged), i...  7.76 us
    pallas_call x1, Pallas kernels, kept_part(): pl.pallas_call(kept_kernel, grid_spec=pltpu.PrefetchScalarGridSpec(num_sc...  7.56 us
    ppermute x1, starting transfers between devices, across_ends(): lax.ppermute(rows, 'section', [(half - 1, sections - 1), (sections - 1, h...  4.91 us
    dynamic_slice x2, local copies, waits for them, and re-layouts, parked_piece(): lax.dynamic_slice(parked_rows, (0, to * share + first * HW), (parked_rows...  3.44 us
  transfers between devices with their start and end apart: 11, of which 8 were waited for; matrix products, arithmetic and copies ran while one was open for 4% of the time, Pallas kernels for 23%

profile of v3, /device:TPU:63, one launch (start us, length us, event | category | flops | bytes accessed | tf_op | source)
XLA Modules:
  0.0 90.8 jit_solution(2435296931635364979)
XLA Ops:
  0.7 2.3 %constant_dynamic-slice_fusion = (bf16[64,2304]{1,0:T(8,128)(2,1)}, bf16[64,2304]{1,0:T(8,128)(2,1)}, bf16[64,2304]{1,0:T(8,128)(2,1)}, bf16[64,2304]{1,0:T(8,128)(2,1)}) fusion(bf16[64,18432]{1,0:T(8,128)(2,1)} %param.6, s32[]{:T(128)S(6)} %select_n.51, s32[]{:T(128)S(6)} %select_n.47, s32[]{:T(128)S(6)} %select_n.46, s32[]{:T(128)S(6)} %select_n.50), kind=kLoop, calls=%fused_computation | loop fusion | bytes 2359312 | tf_op jit(solution)/shard_map/dynamic_slice | solution.py:294
  3.0 5.6 %collective-permute-start.3 = (bf16[64,2304]{1,0:T(8,128)(2,1)}, bf16[64,2304]{1,0:T(8,128)(2,1)}, u32[]{:S(2)}, u32[]{:S(2)}) collective-permute-start(bf16[64,2304]{1,0:T(8,128)(2,1)} %get-tuple-element.18), channel_id=1, source_target_pairs={{0,130},{1,131},{2,128},{3,129},{4,134},{5,135},{6,132},{7,133},{8... | collective-permute-start | bytes 884744 | tf_op jit(solution)/shard_map/ppermute | solution.py:280
  8.6 1.1 %constant_dynamic-slice_fusion.2 = (bf16[64,4608]{1,0:T(8,128)(2,1)}, bf16[64,4608]{1,0:T(8,128)(2,1)}) fusion(bf16[64,18432]{1,0:T(8,128)(2,1)S(1)} %copy-done.2, s32[]{:T(128)S(6)} %select_n.49, s32[]{:T(128)S(6)} %select_n.48), kind=kLoop, calls=%fused_computation.2 | loop fusion | bytes 2359304 | tf_op jit(solution)/shard_map/dynamic_slice | solution.py:294
  9.7 0.7 collective-permute-start.5
  10.4 0.7 collective-permute-start.4
  11.8 7.6 %kept_grads.1 = (bf16[256,4608]{1,0:T(8,128)(2,1)S(1)}, bf16[128,4608]{1,0:T(8,128)(2,1)S(1)}) custom-call(s32[3]{0:T(128)S(1)} %copy-done, s32[1]{0:T(128)S(6)} %copy.10.evicted, bf16[384,4608]{1,0:T(8,128)(2,1)} %rows.1, bf16[512,1536]{1,0:T(8,128)(2,1)} %g1.5, bf16[512,1536]{1,0:T(8,128)(2,1)} %g1.5, bf16[512,1536]{1,0:T(8,128)(2,1)} %g1.5), custom_call_target="tpu_custom_call" | custom-call | flops 12000000000 | bytes 1048576 | tf_op jit(solution)/shard_map/kept_grads/pallas_call | solution.py:151
  19.4 1.0 %copy-done.1 = bf16[128,4608]{1,0:T(8,128)(2,1)} copy-done((bf16[128,4608]{1,0:T(8,128)(2,1)}, bf16[128,4608]{1,0:T(8,128)(2,1)S(1)}, u32[]{:S(2)}) %copy-start.1) | copy-done | bytes 1179672
  20.4 1.2 %collective-permute-start.1 = (bf16[256,4608]{1,0:T(8,128)(2,1)S(1)}, bf16[256,4608]{1,0:T(8,128)(2,1)S(1)}, u32[]{:S(2)}, u32[]{:S(2)}) collective-permute-start(bf16[256,4608]{1,0:T(8,128)(2,1)S(1)} %get-tuple-element.12), channel_id=1, source_target_pairs={{0,124},{4,0},{8,4},{12,8},{16,12},{20,16},{24,20},{28,24},{32,28}... | collective-permute-start | bytes 7077896 | tf_op jit(solution)/shard_map/ppermute | solution.py:284
  21.7 5.1 %collective-permute-done.3.r1 = bf16[64,2304]{1,0:T(8,128)(2,1)} collective-permute-done((bf16[64,2304]{1,0:T(8,128)(2,1)}, bf16[64,2304]{1,0:T(8,128)(2,1)}, u32[]{:S(2)}, u32[]{:S(2)}) %collective-permute-start.3) | collective-permute-done | bytes 294944 | tf_op jit(solution)/shard_map/ppermute | solution.py:280
  26.8 3.3 %collective-permute-start.8 = (bf16[64,2304]{1,0:T(8,128)(2,1)}, bf16[64,2304]{1,0:T(8,128)(2,1)S(1)}, u32[]{:S(2)}, u32[]{:S(2)}) collective-permute-start(bf16[64,2304]{1,0:T(8,128)(2,1)} %get-tuple-element.17), channel_id=1, source_target_pairs={{0,130},{1,131},{2,128},{3,129},{4,134},{5,135},{6,132},{7,133},{8... | collective-permute-start | bytes 884744 | tf_op jit(solution)/shard_map/ppermute | solution.py:280
  30.2 1.8 %collective-permute-done.2.r0 = bf16[64,2304]{1,0:T(8,128)(2,1)} collective-permute-done((bf16[64,2304]{1,0:T(8,128)(2,1)}, bf16[64,2304]{1,0:T(8,128)(2,1)}, u32[]{:S(2)}, u32[]{:S(2)}) %collective-permute-start.2) | collective-permute-done | bytes 294944 | tf_op jit(solution)/shard_map/ppermute | solution.py:280
  32.0 6.8 %collective-permute-done.5.r3 = bf16[64,4608]{1,0:T(8,128)(2,1)S(1)} collective-permute-done((bf16[64,4608]{1,0:T(8,128)(2,1)}, bf16[64,4608]{1,0:T(8,128)(2,1)S(1)}, u32[]{:S(2)}, u32[]{:S(2)}) %collective-permute-start.5) | collective-permute-done | bytes 589856 | tf_op jit(solution)/shard_map/ppermute | solution.py:280
  38.7 2.9 %collective-permute-done.4.r2 = bf16[64,4608]{1,0:T(8,128)(2,1)S(1)} collective-permute-done((bf16[64,4608]{1,0:T(8,128)(2,1)}, bf16[64,4608]{1,0:T(8,128)(2,1)S(1)}, u32[]{:S(2)}, u32[]{:S(2)}) %collective-permute-start.4) | collective-permute-done | bytes 589856 | tf_op jit(solution)/shard_map/ppermute | solution.py:280
  41.7 4.2 %parked_grads.2 = bf16[256,2304]{1,0:T(8,128)(2,1)S(1)} custom-call(s32[3]{0:T(128)S(1)} %copy-done, s32[1]{0:T(128)S(6)} %copy.10.evicted, s32[4]{0:T(128)S(1)} %pad_add_fusion.quarters, bf16[64,2304]{1,0:T(8,128)(2,1)} %collective-permute-done.2.r0, bf16[64,2304]{1,0:T(8,128)(2,1)} %collective-permute-done.3.r1, ...), custom_call_target="tpu_custom_call" | custom-call | flops 24000000000 | bytes 1048576 | tf_op jit(solution)/shard_map/parked_grads/pallas_call | solution.py:200
  45.9 6.8 %collective-permute-done.1.refs_0_ = bf16[256,4608]{1,0:T(8,128)(2,1)S(1)} collective-permute-done((bf16[256,4608]{1,0:T(8,128)(2,1)S(1)}, bf16[256,4608]{1,0:T(8,128)(2,1)S(1)}, u32[]{:S(2)}, u32[]{:S(2)}) %collective-permute-start.1) | collective-permute-done | bytes 2359328 | tf_op jit(solution)/shard_map/ppermute | solution.py:284
  52.7 4.9 %collective-permute-start.6 = (bf16[256,4608]{1,0:T(8,128)(2,1)S(1)}, bf16[256,4608]{1,0:T(8,128)(2,1)S(1)}, u32[]{:S(2)}, u32[]{:S(2)}) collective-permute-start(bf16[256,4608]{1,0:T(8,128)(2,1)S(1)} %collective-permute-done.1.refs_0_), channel_id=1, source_target_pairs={{124,252},{252,124},{125,253},{253,125},{126,254},{254,126},{127,2... | collective-permute-start | bytes 7077896 | tf_op jit(solution)/shard_map/ppermute | solution.py:287
  57.7 2.6 %place_rows.3.refs_1_ = bf16[512,4608]{1,0:T(8,128)(2,1)} custom-call(s32[3]{0:T(128)S(1)} %copy-done, s32[1]{0:T(128)} %collective-permute-done.evicted, s32[1]{0:T(128)} %bitcast.flag, bf16[256,4608]{1,0:T(8,128)(2,1)S(1)} %collective-permute-done.1.refs_0_), custom_call_target="tpu_custom_call" | custom-call | flops 1000000000 | bytes 1048576 | tf_op jit(solution)/shard_map/place_rows/pallas_call | solution.py:253
  60.3 2.8 %collective-permute-done.7.r0 = bf16[64,2304]{1,0:T(8,128)(2,1)S(1)} collective-permute-done((bf16[64,2304]{1,0:T(8,128)(2,1)}, bf16[64,2304]{1,0:T(8,128)(2,1)S(1)}, u32[]{:S(2)}, u32[]{:S(2)}) %collective-permute-start.7) | collective-permute-done | bytes 294944 | tf_op jit(solution)/shard_map/ppermute | solution.py:280
  63.0 4.1 %parked_grads.3 = bf16[256,2304]{1,0:T(8,128)(2,1)S(1)} custom-call(s32[3]{0:T(128)S(1)} %copy-done, s32[1]{0:T(128)S(6)} %copy.10.evicted, s32[4]{0:T(128)S(1)} %pad_add_fusion.quarters, bf16[64,2304]{1,0:T(8,128)(2,1)S(1)} %collective-permute-done.7.r0, bf16[64,2304]{1,0:T(8,128)(2,1)S(1)} %collective-permute-done.8.r1, ...), custom_call_target="tpu_custom_call" | custom-call | flops 48000000000 | bytes 1048576 | tf_op jit(solution)/shard_map/parked_grads/pallas_call | solution.py:200
  67.2 1.0 %collective-permute-start.9 = (bf16[256,2304]{1,0:T(8,128)(2,1)S(1)}, bf16[256,2304]{1,0:T(8,128)(2,1)S(1)}, u32[]{:S(2)}, u32[]{:S(2)}) collective-permute-start(bf16[256,2304]{1,0:T(8,128)(2,1)S(1)} %parked_grads.3), channel_id=1, source_target_pairs={{0,252},{4,0},{8,4},{12,8},{16,12},{20,16},{24,20},{28,24},{32,28}... | collective-permute-start | bytes 3538952 | tf_op jit(solution)/shard_map/ppermute | solution.py:284
  68.2 6.9 %collective-permute-done.10.refs_0_ = bf16[256,2304]{1,0:T(8,128)(2,1)S(1)} collective-permute-done((bf16[256,2304]{1,0:T(8,128)(2,1)S(1)}, bf16[256,2304]{1,0:T(8,128)(2,1)S(1)}, u32[]{:S(2)}, u32[]{:S(2)}) %collective-permute-start.10) | collective-permute-done | bytes 1179680 | tf_op jit(solution)/shard_map/ppermute | solution.py:284
  75.0 2.2 %place_rows.4.refs_2_ = bf16[512,4608]{1,0:T(8,128)(2,1)} custom-call(s32[3]{0:T(128)S(1)} %copy-done, s32[1]{0:T(128)} %collective-permute-done.evicted, s32[1]{0:T(128)} %bitcast.flag, bf16[256,2304]{1,0:T(8,128)(2,1)S(1)} %collective-permute-done.10.refs_0_, bf16[512,4608]{1,0:T(8,128)(2,1)} %place_rows.3.refs_1_), custom_call_target="tpu_custom_call", output_to_operand_aliasing={{}: (4, {})} | custom-call | flops 1000000000 | bytes 1048576 | tf_op jit(solution)/shard_map/place_rows/pallas_call | solution.py:253
  77.2 10.4 %collective-permute-done.9.refs_1_ = bf16[256,2304]{1,0:T(8,128)(2,1)S(1)} collective-permute-done((bf16[256,2304]{1,0:T(8,128)(2,1)S(1)}, bf16[256,2304]{1,0:T(8,128)(2,1)S(1)}, u32[]{:S(2)}, u32[]{:S(2)}) %collective-permute-start.9) | collective-permute-done | bytes 1179680 | tf_op jit(solution)/shard_map/ppermute | solution.py:284
  87.7 3.0 %place_rows.5 = bf16[512,4608]{1,0:T(8,128)(2,1)} custom-call(s32[3]{0:T(128)S(1)} %copy-done, s32[1]{0:T(128)} %collective-permute-done.evicted, s32[1]{0:T(128)} %bitcast.flag, bf16[256,4608]{1,0:T(8,128)(2,1)S(1)} %collective-permute-done.6.refs_0_, bf16[256,2304]{1,0:T(8,128)(2,1)S(1)} %collective-permute-done.9.refs_1_, ...), custom_call_target="tpu_custom_call", output_to_operand_aliasing={{}: (5, {})} | custom-call | flops 1000000000 | bytes 1048576 | tf_op jit(solution)/shard_map/place_rows/pallas_call | solution.py:253
  (13 shorter events, 0.8 us)
Async XLA Ops:
  0.0 8.6 %copy-start.2 = (bf16[64,18432]{1,0:T(8,128)(2,1)S(1)}, bf16[64,18432]{1,0:T(8,128)(2,1)}, u32[]{:S(2)}) copy-start(bf16[64,18432]{1,0:T(8,128)(2,1)} %param.6) | copy-start | bytes 7077892
  0.0 20.4 %collective-permute-start = (s32[1]{0:T(128)}, s32[1]{0:T(128)}, u32[]{:S(2)}, u32[]{:S(2)}) collective-permute-start(s32[1]{0:T(128)} %param.9), channel_id=1, source_target_pairs={{0,252},{4,0},{8,4},{12,8},{16,12},{20,16},{24,20},{28,24},{32,28}... | collective-permute-start | bytes 20 | tf_op jit(solution)/shard_map/ppermute | solution.py:284
  0.7 11.1 %copy-start = (s32[3]{0:T(128)S(1)}, s32[3]{0:T(128)}, u32[]{:S(2)}) copy-start(s32[3]{0:T(128)} %lengths.10) | copy-start | bytes 40
  3.0 23.8 %collective-permute-start.3 = (bf16[64,2304]{1,0:T(8,128)(2,1)}, bf16[64,2304]{1,0:T(8,128)(2,1)}, u32[]{:S(2)}, u32[]{:S(2)}) collective-permute-start(bf16[64,2304]{1,0:T(8,128)(2,1)} %get-tuple-element.18), channel_id=1, source_target_pairs={{0,130},{1,131},{2,128},{3,129},{4,134},{5,135},{6,132},{7,133},{8... | collective-permute-start | bytes 884744 | tf_op jit(solution)/shard_map/ppermute | solution.py:280
  8.6 23.4 %collective-permute-start.2 = (bf16[64,2304]{1,0:T(8,128)(2,1)}, bf16[64,2304]{1,0:T(8,128)(2,1)}, u32[]{:S(2)}, u32[]{:S(2)}) collective-permute-start(bf16[64,2304]{1,0:T(8,128)(2,1)} %get-tuple-element.19), channel_id=1, source_target_pairs={{0,129},{1,130},{2,131},{3,128},{4,133},{5,134},{6,135},{7,132},{8... | collective-permute-start | bytes 884744 | tf_op jit(solution)/shard_map/ppermute | solution.py:280
  9.7 29.0 %collective-permute-start.5 = (bf16[64,4608]{1,0:T(8,128)(2,1)}, bf16[64,4608]{1,0:T(8,128)(2,1)S(1)}, u32[]{:S(2)}, u32[]{:S(2)}) collective-permute-start(bf16[64,4608]{1,0:T(8,128)(2,1)} %get-tuple-element.21), channel_id=1, source_target_pairs={{0,131},{1,128},{2,129},{3,130},{4,135},{5,132},{6,133},{7,134},{8... | collective-permute-start | bytes 1769480 | tf_op jit(solution)/shard_map/ppermute | solution.py:280
  10.4 31.2 %collective-permute-start.4 = (bf16[64,4608]{1,0:T(8,128)(2,1)}, bf16[64,4608]{1,0:T(8,128)(2,1)S(1)}, u32[]{:S(2)}, u32[]{:S(2)}) collective-permute-start(bf16[64,4608]{1,0:T(8,128)(2,1)} %get-tuple-element.22), channel_id=1, source_target_pairs={{0,128},{1,129},{2,130},{3,131},{4,132},{5,133},{6,134},{7,135},{8... | collective-permute-start | bytes 1769480 | tf_op jit(solution)/shard_map/ppermute | solution.py:280
  19.4 1.0 %copy-start.1 = (bf16[128,4608]{1,0:T(8,128)(2,1)}, bf16[128,4608]{1,0:T(8,128)(2,1)S(1)}, u32[]{:S(2)}) copy-start(bf16[128,4608]{1,0:T(8,128)(2,1)S(1)} %get-tuple-element.13.third) | copy-start | bytes 3538948
  20.4 32.3 %collective-permute-start.1 = (bf16[256,4608]{1,0:T(8,128)(2,1)S(1)}, bf16[256,4608]{1,0:T(8,128)(2,1)S(1)}, u32[]{:S(2)}, u32[]{:S(2)}) collective-permute-start(bf16[256,4608]{1,0:T(8,128)(2,1)S(1)} %get-tuple-element.12), channel_id=1, source_target_pairs={{0,124},{4,0},{8,4},{12,8},{16,12},{20,16},{24,20},{28,24},{32,28}... | collective-permute-start | bytes 7077896 | tf_op jit(solution)/shard_map/ppermute | solution.py:284
  26.8 33.4 %collective-permute-start.8 = (bf16[64,2304]{1,0:T(8,128)(2,1)}, bf16[64,2304]{1,0:T(8,128)(2,1)S(1)}, u32[]{:S(2)}, u32[]{:S(2)}) collective-permute-start(bf16[64,2304]{1,0:T(8,128)(2,1)} %get-tuple-element.17), channel_id=1, source_target_pairs={{0,130},{1,131},{2,128},{3,129},{4,134},{5,135},{6,132},{7,133},{8... | collective-permute-start | bytes 884744 | tf_op jit(solution)/shard_map/ppermute | solution.py:280
  32.0 31.1 %collective-permute-start.7 = (bf16[64,2304]{1,0:T(8,128)(2,1)}, bf16[64,2304]{1,0:T(8,128)(2,1)S(1)}, u32[]{:S(2)}, u32[]{:S(2)}) collective-permute-start(bf16[64,2304]{1,0:T(8,128)(2,1)} %get-tuple-element.20), channel_id=1, source_target_pairs={{0,129},{1,130},{2,131},{3,128},{4,133},{5,134},{6,135},{7,132},{8... | collective-permute-start | bytes 884744 | tf_op jit(solution)/shard_map/ppermute | solution.py:280
  52.7 22.3 %collective-permute-start.10 = (bf16[256,2304]{1,0:T(8,128)(2,1)S(1)}, bf16[256,2304]{1,0:T(8,128)(2,1)S(1)}, u32[]{:S(2)}, u32[]{:S(2)}) collective-permute-start(bf16[256,2304]{1,0:T(8,128)(2,1)S(1)} %parked_grads.2), channel_id=1, source_target_pairs={{0,252},{4,0},{8,4},{12,8},{16,12},{20,16},{24,20},{28,24},{32,28}... | collective-permute-start | bytes 3538952 | tf_op jit(solution)/shard_map/ppermute | solution.py:284
  52.7 34.9 %collective-permute-start.6 = (bf16[256,4608]{1,0:T(8,128)(2,1)S(1)}, bf16[256,4608]{1,0:T(8,128)(2,1)S(1)}, u32[]{:S(2)}, u32[]{:S(2)}) collective-permute-start(bf16[256,4608]{1,0:T(8,128)(2,1)S(1)} %collective-permute-done.1.refs_0_), channel_id=1, source_target_pairs={{124,252},{252,124},{125,253},{253,125},{126,254},{254,126},{127,2... | collective-permute-start | bytes 7077896 | tf_op jit(solution)/shard_map/ppermute | solution.py:287
  67.2 20.5 %collective-permute-start.9 = (bf16[256,2304]{1,0:T(8,128)(2,1)S(1)}, bf16[256,2304]{1,0:T(8,128)(2,1)S(1)}, u32[]{:S(2)}, u32[]{:S(2)}) collective-permute-start(bf16[256,2304]{1,0:T(8,128)(2,1)S(1)} %parked_grads.3), channel_id=1, source_target_pairs={{0,252},{4,0},{8,4},{12,8},{16,12},{20,16},{24,20},{28,24},{32,28}... | collective-permute-start | bytes 3538952 | tf_op jit(solution)/shard_map/ppermute | solution.py:284

commit v4 on v3

--- a/solution.py
+++ b/solution.py
@@ -18,11 +18,10 @@
 VMEM = 20 << 20
 HOPS = (3, -3, 1, -1)
 KEPT_COST = 1000_000_000
-LATE_COSTS = (8000_000_000,)
+LATE_COST = 8000_000_000
 PLACE_COST = 1000_000_000
 PARKED_COST = 4000_000_000
 PARKED_CHUNKS = (6, 6)
-LAST_CHUNKS = (6,)
 
 
 def pick(index, values):
@@ -162,7 +161,7 @@
         ),
         out_shape=[
             jax.ShapeDtypeStruct((2 * BLK, heads * HW), jnp.bfloat16),
-            jax.ShapeDtypeStruct((BLK, heads * HW), jnp.bfloat16),
+            pltpu.HBM((BLK, heads * HW), jnp.bfloat16),
         ],
         compiler_params=pltpu.CompilerParams(vmem_limit_bytes=VMEM),
         cost_estimate=worth(heads * KEPT_COST),
@@ -170,7 +169,7 @@
     )(lengths, evicted, in_hbm(kept_rows), *[in_hbm(grad_out)] * 3)
 
 
-def parked_kernel(ats, lengths, evicted, quarters, r0, r1, r2, r3, g0, g1, third, late, rows):
+def parked_kernel(ats, lengths, evicted, quarters, r0, r1, r2, r3, g0, g1, third, late0, late1, rows):
     plan = Plan(lengths, evicted)
     quarter = BLK // 2
     for d, piece in enumerate((r0, r1, r2, r3)):
@@ -185,8 +184,8 @@
         grads = [g[:, head * HD : (head + 1) * HD] for g in (g0, g1)]
         grads[1] = jnp.where(plan.long, grads[1], jnp.zeros((), jnp.bfloat16))
         for part, made in enumerate(attention_grads(q, k, v, grads, valids, joins)):
-            late[0:BLK, columns(head, part)] = made[0]
-            late[BLK : 2 * BLK, columns(head, part)] = jnp.where(
+            late0[:, columns(head, part)] = made[0]
+            late1[:, columns(head, part)] = jnp.where(
                 plan.long, made[1], third[:, columns(head, part)]
             )
 
@@ -205,10 +204,10 @@
             in_specs=[pl.BlockSpec(memory_space=pltpu.VMEM)] * 4
             + [grad_spec(j) for j in range(2)]
             + [pl.BlockSpec((BLK, step * HW), lambda i, ln, ev, sh: (0, at + i))],
-            out_specs=pl.BlockSpec((2 * BLK, step * HW), lambda i, ln, ev, sh: (0, i)),
+            out_specs=[pl.BlockSpec((BLK, step * HW), lambda i, ln, ev, sh: (0, i))] * 2,
             scratch_shapes=[pltpu.VMEM((2 * BLK, step * HW), jnp.bfloat16)],
         ),
-        out_shape=jax.ShapeDtypeStruct((2 * BLK, heads * HW), jnp.bfloat16),
+        out_shape=[jax.ShapeDtypeStruct((BLK, heads * HW), jnp.bfloat16)] * 2,
         compiler_params=pltpu.CompilerParams(vmem_limit_bytes=VMEM),
         cost_estimate=worth(heads * flops),
         name="parked_grads",
@@ -229,11 +228,11 @@
         )
 
     def begin(n):
-        for slot in range(2):
+        for slot in range(pieces[n].shape[0] // BLK):
             store(n, slot).start()
 
     def finish(n):
-        for slot in range(2):
+        for slot in range(pieces[n].shape[0] // BLK):
             store(n, slot).wait()
 
     for step in (begin, finish):
@@ -308,19 +307,17 @@
     early, third = kept_part(lengths, evicted, kept_rows, grad_out, 0, p1 + p2)
     x1 = passed_back(once(early, next_evicted), half)
     late1 = parked_part(lengths, evicted, quarters, z1 + both, grad_out, third, 0, p1, PARKED_COST)
-    x2 = passed_back(once(late1, x1))
-    x1_ends = across_ends(once(x1, late1))
+    x2 = [passed_back(rows) for rows in late1]
+    x1_ends = across_ends(once(x1, *late1))
     out = place(lengths, next_evicted, last, None, total, (x1, Plan.kept, 0, False))
-    pieces = []
-    before, first = (late1, out), p1
-    for heads, flops in zip(LAST_CHUNKS, LATE_COSTS):
-        late = parked_part(
-            once(lengths, *before), evicted, quarters, z2 + both, grad_out, third, first, heads, flops, p1
-        )
-        pieces.append((passed_back(late), Plan.late, first, False))
-        before, first = (late, x2), first + heads
-    out = place(lengths, next_evicted, last, out, total, (x2, Plan.late, 0, False))
-    return place(lengths, next_evicted, last, out, total, (x1_ends, Plan.kept, 0, True), *pieces)
+    late2 = parked_part(
+        once(lengths, *late1, out), evicted, quarters, z2 + both, grad_out, third, p1, p2, LATE_COST, p1
+    )
+    x3 = [passed_back(rows) for rows in late2]
+    slots = (lambda plan, slot: plan.late(0), lambda plan, slot: plan.late(1))
+    pieces = lambda rows, first: [(part, to, first, False) for part, to in zip(rows, slots)]
+    out = place(lengths, next_evicted, last, out, total, *pieces(x2, 0))
+    return place(lengths, next_evicted, last, out, total, (x1_ends, Plan.kept, 0, True), *pieces(x3, p1))
 
 
 def solution(mesh):

time: 92.4 us -> 90.7 us (0.982); the launches traced: 90.8 us -> 90.4 us
  waiting for transfers between devices: 43.6 us -> 40.2 us
  starting transfers between devices: 18.1 us -> 21.3 us
  local copies, waits for them, and re-layouts: 4.47 us -> 3.46 us
    ppermute x4 -> x6, waiting for transfers between devices: 24.1 us -> 19.9 us  [passed_back(): return lax.ppermute(rows, 'section', pairs)]
    ppermute x4 -> x6, starting transfers between devices: 2.86 us -> 5.7 us  [passed_back(): return lax.ppermute(rows, 'section', pairs)]
    ppermute x6, starting transfers between devices: 10.4 us -> 11.6 us  [shifted(): return lax.ppermute(rows, ('section', 'tp'), pairs)]
    unnamed x6 -> x4, local copies, waits for them, and re-layouts: 1.03 us -> 0.01 us
  transfers between devices with their start and end apart: 11 -> 13, of which waited for: 8 -> 9; matrix products, arithmetic and copies ran while one was open for 4% -> 4% of each run, Pallas kernels for 23% -> 24%
where the time goes in v4:
time: 90.7 us; the launch traced here: 90.4 us
  waiting for transfers between devices  40.2 us (44%)
  Pallas kernels  24.4 us (27%)
  starting transfers between devices  21.3 us (23%)
  local copies, waits for them, and re-layouts  3.46 us (4%)
    ppermute x6, waiting for transfers between devices, shifted(): return lax.ppermute(rows, ('section', 'tp'), pairs)  20.3 us
    ppermute x6, waiting for transfers between devices, passed_back(): return lax.ppermute(rows, 'section', pairs)  19.9 us
    ppermute x6, starting transfers between devices, shifted(): return lax.ppermute(rows, ('section', 'tp'), pairs)  11.6 us
    pallas_call x2, Pallas kernels, parked_part(): pl.pallas_call(functools.partial(parked_kernel, (far_at, far_at, at, at))...  8.38 us
    pallas_call x1, Pallas kernels, kept_part(): pl.pallas_call(kept_kernel, grid_spec=pltpu.PrefetchScalarGridSpec(num_sc...  8.21 us
    pallas_call x3, Pallas kernels, place(): pl.pallas_call(functools.partial(place_kernel, slots, firsts, flagged), i...  7.85 us
    ppermute x6, starting transfers between devices, passed_back(): return lax.ppermute(rows, 'section', pairs)  5.7 us
    ppermute x1, starting transfers between devices, across_ends(): lax.ppermute(rows, 'section', [(half - 1, sections - 1), (sections - 1, h...  4.01 us
  transfers between devices with their start and end apart: 13, of which 9 were waited for; matrix products, arithmetic and copies ran while one was open for 4% of the time, Pallas kernels for 24%

profile of v4, /device:TPU:63, one launch (start us, length us, event | category | flops | bytes accessed | tf_op | source)
XLA Modules:
  0.0 90.4 jit_solution(3446131439313236052)
XLA Ops:
  0.7 2.3 %constant_dynamic-slice_fusion = (bf16[64,2304]{1,0:T(8,128)(2,1)}, bf16[64,2304]{1,0:T(8,128)(2,1)}, bf16[64,2304]{1,0:T(8,128)(2,1)}, bf16[64,2304]{1,0:T(8,128)(2,1)}) fusion(bf16[64,18432]{1,0:T(8,128)(2,1)} %param.6, s32[]{:T(128)S(6)} %select_n.51, s32[]{:T(128)S(6)} %select_n.47, s32[]{:T(128)S(6)} %select_n.46, s32[]{:T(128)S(6)} %select_n.50), kind=kLoop, calls=%fused_computation | loop fusion | bytes 2359312 | tf_op jit(solution)/shard_map/dynamic_slice | solution.py:293
  3.0 5.6 %collective-permute-start.2 = (bf16[64,2304]{1,0:T(8,128)(2,1)}, bf16[64,2304]{1,0:T(8,128)(2,1)}, u32[]{:S(2)}, u32[]{:S(2)}) collective-permute-start(bf16[64,2304]{1,0:T(8,128)(2,1)} %get-tuple-element.25), channel_id=1, source_target_pairs={{0,129},{1,130},{2,131},{3,128},{4,133},{5,134},{6,135},{7,132},{8... | collective-permute-start | bytes 884744 | tf_op jit(solution)/shard_map/ppermute | solution.py:279
  8.6 1.1 %constant_dynamic-slice_fusion.2 = (bf16[64,4608]{1,0:T(8,128)(2,1)}, bf16[64,4608]{1,0:T(8,128)(2,1)}) fusion(bf16[64,18432]{1,0:T(8,128)(2,1)S(1)} %copy-done.1, s32[]{:T(128)S(6)} %select_n.49, s32[]{:T(128)S(6)} %select_n.48), kind=kLoop, calls=%fused_computation.2 | loop fusion | bytes 2359304 | tf_op jit(solution)/shard_map/dynamic_slice | solution.py:293
  11.8 8.2 %kept_grads.1 = (bf16[256,4608]{1,0:T(8,128)(2,1)S(1)}, bf16[128,4608]{1,0:T(8,128)(2,1)}) custom-call(s32[3]{0:T(128)S(1)} %copy-done, s32[1]{0:T(128)S(6)} %copy.10.evicted, bf16[384,4608]{1,0:T(8,128)(2,1)} %rows.1, bf16[512,1536]{1,0:T(8,128)(2,1)} %g1.5, bf16[512,1536]{1,0:T(8,128)(2,1)} %g1.5, bf16[512,1536]{1,0:T(8,128)(2,1)} %g1.5), custom_call_target="tpu_custom_call" | custom-call | flops 12000000000 | bytes 1048576 | tf_op jit(solution)/shard_map/kept_grads/pallas_call | solution.py:150
  20.1 1.2 %collective-permute-start.1 = (bf16[256,4608]{1,0:T(8,128)(2,1)S(1)}, bf16[256,4608]{1,0:T(8,128)(2,1)S(1)}, u32[]{:S(2)}, u32[]{:S(2)}) collective-permute-start(bf16[256,4608]{1,0:T(8,128)(2,1)S(1)} %get-tuple-element.15), channel_id=1, source_target_pairs={{0,124},{4,0},{8,4},{12,8},{16,12},{20,16},{24,20},{28,24},{32,28}... | collective-permute-start | bytes 7077896 | tf_op jit(solution)/shard_map/ppermute | solution.py:283
  21.3 6.5 %collective-permute-done.2.r0 = bf16[64,2304]{1,0:T(8,128)(2,1)} collective-permute-done((bf16[64,2304]{1,0:T(8,128)(2,1)}, bf16[64,2304]{1,0:T(8,128)(2,1)}, u32[]{:S(2)}, u32[]{:S(2)}) %collective-permute-start.2) | collective-permute-done | bytes 294944 | tf_op jit(solution)/shard_map/ppermute | solution.py:279
  27.8 2.9 %collective-permute-start.7 = (bf16[64,2304]{1,0:T(8,128)(2,1)}, bf16[64,2304]{1,0:T(8,128)(2,1)S(1)}, u32[]{:S(2)}, u32[]{:S(2)}) collective-permute-start(bf16[64,2304]{1,0:T(8,128)(2,1)} %get-tuple-element.26), channel_id=1, source_target_pairs={{0,129},{1,130},{2,131},{3,128},{4,133},{5,134},{6,135},{7,132},{8... | collective-permute-start | bytes 884744 | tf_op jit(solution)/shard_map/ppermute | solution.py:279
  30.8 1.7 %collective-permute-start.8 = (bf16[64,2304]{1,0:T(8,128)(2,1)}, bf16[64,2304]{1,0:T(8,128)(2,1)S(1)}, u32[]{:S(2)}, u32[]{:S(2)}) collective-permute-start(bf16[64,2304]{1,0:T(8,128)(2,1)} %get-tuple-element.23), channel_id=1, source_target_pairs={{0,130},{1,131},{2,128},{3,129},{4,134},{5,135},{6,132},{7,133},{8... | collective-permute-start | bytes 884744 | tf_op jit(solution)/shard_map/ppermute | solution.py:279
  32.4 7.3 %collective-permute-done.4.r2 = bf16[64,4608]{1,0:T(8,128)(2,1)S(1)} collective-permute-done((bf16[64,4608]{1,0:T(8,128)(2,1)}, bf16[64,4608]{1,0:T(8,128)(2,1)S(1)}, u32[]{:S(2)}, u32[]{:S(2)}) %collective-permute-start.4) | collective-permute-done | bytes 589856 | tf_op jit(solution)/shard_map/ppermute | solution.py:279
  39.7 2.3 %collective-permute-done.5.r3 = bf16[64,4608]{1,0:T(8,128)(2,1)S(1)} collective-permute-done((bf16[64,4608]{1,0:T(8,128)(2,1)}, bf16[64,4608]{1,0:T(8,128)(2,1)S(1)}, u32[]{:S(2)}, u32[]{:S(2)}) %collective-permute-start.5) | collective-permute-done | bytes 589856 | tf_op jit(solution)/shard_map/ppermute | solution.py:279
  42.0 4.2 %parked_grads.2 = (bf16[128,2304]{1,0:T(8,128)(2,1)S(1)}, bf16[128,2304]{1,0:T(8,128)(2,1)S(1)}) custom-call(s32[3]{0:T(128)S(1)} %copy-done, s32[1]{0:T(128)S(6)} %copy.10.evicted, s32[4]{0:T(128)S(1)} %pad_add_fusion.quarters, bf16[64,2304]{1,0:T(8,128)(2,1)} %collective-permute-done.2.r0, bf16[64,2304]{1,0:T(8,128)(2,1)} %collective-permute-done.3.r1, ...), custom_call_target="tpu_custom_call" | custom-call | flops 24000000000 | bytes 1048576 | tf_op jit(solution)/shard_map/parked_grads/pallas_call | solution.py:199
  46.3 2.3 %collective-permute-start.11 = (bf16[128,2304]{1,0:T(8,128)(2,1)S(1)}, bf16[128,2304]{1,0:T(8,128)(2,1)S(1)}, u32[]{:S(2)}, u32[]{:S(2)}) collective-permute-start(bf16[128,2304]{1,0:T(8,128)(2,1)S(1)} %get-tuple-element.17), channel_id=1, source_target_pairs={{0,252},{4,0},{8,4},{12,8},{16,12},{20,16},{24,20},{28,24},{32,28}... | collective-permute-start | bytes 1769480 | tf_op jit(solution)/shard_map/ppermute | solution.py:283
  48.6 3.7 %collective-permute-done.1.refs_0_ = bf16[256,4608]{1,0:T(8,128)(2,1)S(1)} collective-permute-done((bf16[256,4608]{1,0:T(8,128)(2,1)S(1)}, bf16[256,4608]{1,0:T(8,128)(2,1)S(1)}, u32[]{:S(2)}, u32[]{:S(2)}) %collective-permute-start.1) | collective-permute-done | bytes 2359328 | tf_op jit(solution)/shard_map/ppermute | solution.py:283
  52.4 4.0 %collective-permute-start.6 = (bf16[256,4608]{1,0:T(8,128)(2,1)S(1)}, bf16[256,4608]{1,0:T(8,128)(2,1)S(1)}, u32[]{:S(2)}, u32[]{:S(2)}) collective-permute-start(bf16[256,4608]{1,0:T(8,128)(2,1)S(1)} %collective-permute-done.1.refs_0_), channel_id=1, source_target_pairs={{124,252},{252,124},{125,253},{253,125},{126,254},{254,126},{127,2... | collective-permute-start | bytes 7077896 | tf_op jit(solution)/shard_map/ppermute | solution.py:286
  56.4 2.6 %place_rows.3.refs_2_ = bf16[512,4608]{1,0:T(8,128)(2,1)} custom-call(s32[3]{0:T(128)S(1)} %copy-done, s32[1]{0:T(128)} %collective-permute-done.evicted, s32[1]{0:T(128)} %bitcast.flag, bf16[256,4608]{1,0:T(8,128)(2,1)S(1)} %collective-permute-done.1.refs_0_), custom_call_target="tpu_custom_call" | custom-call | flops 1000000000 | bytes 1048576 | tf_op jit(solution)/shard_map/place_rows/pallas_call | solution.py:252
  59.0 1.2 %collective-permute-done.7.r0 = bf16[64,2304]{1,0:T(8,128)(2,1)S(1)} collective-permute-done((bf16[64,2304]{1,0:T(8,128)(2,1)}, bf16[64,2304]{1,0:T(8,128)(2,1)S(1)}, u32[]{:S(2)}, u32[]{:S(2)}) %collective-permute-start.7) | collective-permute-done | bytes 294944 | tf_op jit(solution)/shard_map/ppermute | solution.py:279
  60.1 3.0 %collective-permute-done.8.r1 = bf16[64,2304]{1,0:T(8,128)(2,1)S(1)} collective-permute-done((bf16[64,2304]{1,0:T(8,128)(2,1)}, bf16[64,2304]{1,0:T(8,128)(2,1)S(1)}, u32[]{:S(2)}, u32[]{:S(2)}) %collective-permute-start.8) | collective-permute-done | bytes 294944 | tf_op jit(solution)/shard_map/ppermute | solution.py:279
  63.1 4.1 %parked_grads.3 = (bf16[128,2304]{1,0:T(8,128)(2,1)S(1)}, bf16[128,2304]{1,0:T(8,128)(2,1)S(1)}) custom-call(s32[3]{0:T(128)S(1)} %copy-done, s32[1]{0:T(128)S(6)} %copy.10.evicted, s32[4]{0:T(128)S(1)} %pad_add_fusion.quarters, bf16[64,2304]{1,0:T(8,128)(2,1)S(1)} %collective-permute-done.7.r0, bf16[64,2304]{1,0:T(8,128)(2,1)S(1)} %collective-permute-done.8.r1, ...), custom_call_target="tpu_custom_call" | custom-call | flops 48000000000 | bytes 1048576 | tf_op jit(solution)/shard_map/parked_grads/pallas_call | solution.py:199
  67.3 1.3 %collective-permute-start.9 = (bf16[128,2304]{1,0:T(8,128)(2,1)S(1)}, bf16[128,2304]{1,0:T(8,128)(2,1)S(1)}, u32[]{:S(2)}, u32[]{:S(2)}) collective-permute-start(bf16[128,2304]{1,0:T(8,128)(2,1)S(1)} %get-tuple-element.21), channel_id=1, source_target_pairs={{0,252},{4,0},{8,4},{12,8},{16,12},{20,16},{24,20},{28,24},{32,28}... | collective-permute-start | bytes 1769480 | tf_op jit(solution)/shard_map/ppermute | solution.py:283
  68.8 2.5 %collective-permute-done.12.refs_1_ = bf16[128,2304]{1,0:T(8,128)(2,1)S(1)} collective-permute-done((bf16[128,2304]{1,0:T(8,128)(2,1)S(1)}, bf16[128,2304]{1,0:T(8,128)(2,1)S(1)}, u32[]{:S(2)}, u32[]{:S(2)}) %collective-permute-start.12) | collective-permute-done | bytes 589856 | tf_op jit(solution)/shard_map/ppermute | solution.py:283
  71.3 2.2 %place_rows.4.refs_3_ = bf16[512,4608]{1,0:T(8,128)(2,1)} custom-call(s32[3]{0:T(128)S(1)} %copy-done, s32[1]{0:T(128)} %collective-permute-done.evicted, s32[1]{0:T(128)} %bitcast.flag, bf16[128,2304]{1,0:T(8,128)(2,1)S(1)} %collective-permute-done.11.refs_0_, ...), custom_call_target="tpu_custom_call", output_to_operand_aliasing={{}: (5, {})} | custom-call | flops 1000000000 | bytes 1048576 | tf_op jit(solution)/shard_map/place_rows/pallas_call | solution.py:252
  73.5 7.4 %collective-permute-done.9.refs_1_ = bf16[128,2304]{1,0:T(8,128)(2,1)S(1)} collective-permute-done((bf16[128,2304]{1,0:T(8,128)(2,1)S(1)}, bf16[128,2304]{1,0:T(8,128)(2,1)S(1)}, u32[]{:S(2)}, u32[]{:S(2)}) %collective-permute-start.9) | collective-permute-done | bytes 589856 | tf_op jit(solution)/shard_map/ppermute | solution.py:283
  80.9 6.3 %collective-permute-done.10.refs_2_ = bf16[128,2304]{1,0:T(8,128)(2,1)S(1)} collective-permute-done((bf16[128,2304]{1,0:T(8,128)(2,1)S(1)}, bf16[128,2304]{1,0:T(8,128)(2,1)S(1)}, u32[]{:S(2)}, u32[]{:S(2)}) %collective-permute-start.10) | collective-permute-done | bytes 589856 | tf_op jit(solution)/shard_map/ppermute | solution.py:283
  87.2 3.0 %place_rows.5 = bf16[512,4608]{1,0:T(8,128)(2,1)} custom-call(s32[3]{0:T(128)S(1)} %copy-done, s32[1]{0:T(128)} %collective-permute-done.evicted, s32[1]{0:T(128)} %bitcast.flag, bf16[256,4608]{1,0:T(8,128)(2,1)S(1)} %collective-permute-done.6.refs_0_, bf16[128,2304]{1,0:T(8,128)(2,1)S(1)} %collective-permute-done.9.refs_1_, ...), custom_call_target="tpu_custom_call", output_to_operand_aliasing={{}: (6, {})} | custom-call | flops 1000000000 | bytes 1048576 | tf_op jit(solution)/shard_map/place_rows/pallas_call | solution.py:252
  (15 shorter events, 2.6 us)
Async XLA Ops:
  0.0 8.6 %copy-start.1 = (bf16[64,18432]{1,0:T(8,128)(2,1)S(1)}, bf16[64,18432]{1,0:T(8,128)(2,1)}, u32[]{:S(2)}) copy-start(bf16[64,18432]{1,0:T(8,128)(2,1)} %param.6) | copy-start | bytes 7077892
  0.0 20.1 %collective-permute-start = (s32[1]{0:T(128)}, s32[1]{0:T(128)}, u32[]{:S(2)}, u32[]{:S(2)}) collective-permute-start(s32[1]{0:T(128)} %param.9), channel_id=1, source_target_pairs={{0,252},{4,0},{8,4},{12,8},{16,12},{20,16},{24,20},{28,24},{32,28}... | collective-permute-start | bytes 20 | tf_op jit(solution)/shard_map/ppermute | solution.py:283
  0.7 11.2 %copy-start = (s32[3]{0:T(128)S(1)}, s32[3]{0:T(128)}, u32[]{:S(2)}) copy-start(s32[3]{0:T(128)} %lengths.10) | copy-start | bytes 40
  3.0 24.8 %collective-permute-start.2 = (bf16[64,2304]{1,0:T(8,128)(2,1)}, bf16[64,2304]{1,0:T(8,128)(2,1)}, u32[]{:S(2)}, u32[]{:S(2)}) collective-permute-start(bf16[64,2304]{1,0:T(8,128)(2,1)} %get-tuple-element.25), channel_id=1, source_target_pairs={{0,129},{1,130},{2,131},{3,128},{4,133},{5,134},{6,135},{7,132},{8... | collective-permute-start | bytes 884744 | tf_op jit(solution)/shard_map/ppermute | solution.py:279
  8.6 22.2 %collective-permute-start.3 = (bf16[64,2304]{1,0:T(8,128)(2,1)}, bf16[64,2304]{1,0:T(8,128)(2,1)}, u32[]{:S(2)}, u32[]{:S(2)}) collective-permute-start(bf16[64,2304]{1,0:T(8,128)(2,1)} %get-tuple-element.24), channel_id=1, source_target_pairs={{0,130},{1,131},{2,128},{3,129},{4,134},{5,135},{6,132},{7,133},{8... | collective-permute-start | bytes 884744 | tf_op jit(solution)/shard_map/ppermute | solution.py:279
  9.7 30.0 %collective-permute-start.4 = (bf16[64,4608]{1,0:T(8,128)(2,1)}, bf16[64,4608]{1,0:T(8,128)(2,1)S(1)}, u32[]{:S(2)}, u32[]{:S(2)}) collective-permute-start(bf16[64,4608]{1,0:T(8,128)(2,1)} %get-tuple-element.28), channel_id=1, source_target_pairs={{0,128},{1,129},{2,130},{3,131},{4,132},{5,133},{6,134},{7,135},{8... | collective-permute-start | bytes 1769480 | tf_op jit(solution)/shard_map/ppermute | solution.py:279
  10.4 31.6 %collective-permute-start.5 = (bf16[64,4608]{1,0:T(8,128)(2,1)}, bf16[64,4608]{1,0:T(8,128)(2,1)S(1)}, u32[]{:S(2)}, u32[]{:S(2)}) collective-permute-start(bf16[64,4608]{1,0:T(8,128)(2,1)} %get-tuple-element.27), channel_id=1, source_target_pairs={{0,131},{1,128},{2,129},{3,130},{4,135},{5,132},{6,133},{7,134},{8... | collective-permute-start | bytes 1769480 | tf_op jit(solution)/shard_map/ppermute | solution.py:279
  20.1 32.3 %collective-permute-start.1 = (bf16[256,4608]{1,0:T(8,128)(2,1)S(1)}, bf16[256,4608]{1,0:T(8,128)(2,1)S(1)}, u32[]{:S(2)}, u32[]{:S(2)}) collective-permute-start(bf16[256,4608]{1,0:T(8,128)(2,1)S(1)} %get-tuple-element.15), channel_id=1, source_target_pairs={{0,124},{4,0},{8,4},{12,8},{16,12},{20,16},{24,20},{28,24},{32,28}... | collective-permute-start | bytes 7077896 | tf_op jit(solution)/shard_map/ppermute | solution.py:283
  27.8 32.3 %collective-permute-start.7 = (bf16[64,2304]{1,0:T(8,128)(2,1)}, bf16[64,2304]{1,0:T(8,128)(2,1)S(1)}, u32[]{:S(2)}, u32[]{:S(2)}) collective-permute-start(bf16[64,2304]{1,0:T(8,128)(2,1)} %get-tuple-element.26), channel_id=1, source_target_pairs={{0,129},{1,130},{2,131},{3,128},{4,133},{5,134},{6,135},{7,132},{8... | collective-permute-start | bytes 884744 | tf_op jit(solution)/shard_map/ppermute | solution.py:279
  30.8 32.4 %collective-permute-start.8 = (bf16[64,2304]{1,0:T(8,128)(2,1)}, bf16[64,2304]{1,0:T(8,128)(2,1)S(1)}, u32[]{:S(2)}, u32[]{:S(2)}) collective-permute-start(bf16[64,2304]{1,0:T(8,128)(2,1)} %get-tuple-element.23), channel_id=1, source_target_pairs={{0,130},{1,131},{2,128},{3,129},{4,134},{5,135},{6,132},{7,133},{8... | collective-permute-start | bytes 884744 | tf_op jit(solution)/shard_map/ppermute | solution.py:279
  46.3 22.5 %collective-permute-start.11 = (bf16[128,2304]{1,0:T(8,128)(2,1)S(1)}, bf16[128,2304]{1,0:T(8,128)(2,1)S(1)}, u32[]{:S(2)}, u32[]{:S(2)}) collective-permute-start(bf16[128,2304]{1,0:T(8,128)(2,1)S(1)} %get-tuple-element.17), channel_id=1, source_target_pairs={{0,252},{4,0},{8,4},{12,8},{16,12},{20,16},{24,20},{28,24},{32,28}... | collective-permute-start | bytes 1769480 | tf_op jit(solution)/shard_map/ppermute | solution.py:283
  48.5 22.7 %collective-permute-start.12 = (bf16[128,2304]{1,0:T(8,128)(2,1)S(1)}, bf16[128,2304]{1,0:T(8,128)(2,1)S(1)}, u32[]{:S(2)}, u32[]{:S(2)}) collective-permute-start(bf16[128,2304]{1,0:T(8,128)(2,1)S(1)} %get-tuple-element.18), channel_id=1, source_target_pairs={{0,252},{4,0},{8,4},{12,8},{16,12},{20,16},{24,20},{28,24},{32,28}... | collective-permute-start | bytes 1769480 | tf_op jit(solution)/shard_map/ppermute | solution.py:283
  52.4 34.8 %collective-permute-start.6 = (bf16[256,4608]{1,0:T(8,128)(2,1)S(1)}, bf16[256,4608]{1,0:T(8,128)(2,1)S(1)}, u32[]{:S(2)}, u32[]{:S(2)}) collective-permute-start(bf16[256,4608]{1,0:T(8,128)(2,1)S(1)} %collective-permute-done.1.refs_0_), channel_id=1, source_target_pairs={{124,252},{252,124},{125,253},{253,125},{126,254},{254,126},{127,2... | collective-permute-start | bytes 7077896 | tf_op jit(solution)/shard_map/ppermute | solution.py:286
  67.3 13.6 %collective-permute-start.9 = (bf16[128,2304]{1,0:T(8,128)(2,1)S(1)}, bf16[128,2304]{1,0:T(8,128)(2,1)S(1)}, u32[]{:S(2)}, u32[]{:S(2)}) collective-permute-start(bf16[128,2304]{1,0:T(8,128)(2,1)S(1)} %get-tuple-element.21), channel_id=1, source_target_pairs={{0,252},{4,0},{8,4},{12,8},{16,12},{20,16},{24,20},{28,24},{32,28}... | collective-permute-start | bytes 1769480 | tf_op jit(solution)/shard_map/ppermute | solution.py:283
  68.5 18.7 %collective-permute-start.10 = (bf16[128,2304]{1,0:T(8,128)(2,1)S(1)}, bf16[128,2304]{1,0:T(8,128)(2,1)S(1)}, u32[]{:S(2)}, u32[]{:S(2)}) collective-permute-start(bf16[128,2304]{1,0:T(8,128)(2,1)S(1)} %get-tuple-element.22), channel_id=1, source_target_pairs={{0,252},{4,0},{8,4},{12,8},{16,12},{20,16},{24,20},{28,24},{32,28}... | collective-permute-start | bytes 1769480 | tf_op jit(solution)/shard_map/ppermute | solution.py:283

commit v5 on v4

--- a/solution.py
+++ b/solution.py
@@ -285,15 +285,16 @@
     def across_ends(rows):
         return lax.ppermute(rows, "section", [(half - 1, sections - 1), (sections - 1, half - 1)])
 
-    next_evicted = passed_back(evicted)
     last = (lax.rem(lax.axis_index("section"), half) == half - 1).astype(jnp.int32).reshape(1)
 
-    def parked_piece(hops, first, heads):
+    def parked_slice(hops, first, heads):
         to = lax.rem(spot + hops + ring, ring) // 2
-        rows = lax.dynamic_slice(
+        return lax.dynamic_slice(
             parked_rows, (0, to * share + first * HW), (parked_rows.shape[0], heads * HW)
         )
-        return shifted(rows, hops)
+
+    def parked_piece(hops, first, heads):
+        return shifted(parked_slice(hops, first, heads), hops)
 
     def once(value, *done):
         return lax.optimization_barrier((value, *done))[0]
@@ -301,7 +302,9 @@
     quarters = jnp.stack([lax.rem(spot - hops + ring, ring) // 2 for hops in HOPS]).astype(jnp.int32)
     p1, p2 = PARKED_CHUNKS
     far, near = HOPS[:2], HOPS[2:]
-    z1 = [parked_piece(hops, 0, p1) for hops in far]
+    far_rows = [parked_slice(hops, 0, p1) for hops in far]
+    z1 = [shifted(rows, hops) for rows, hops in zip(far_rows, far)]
+    next_evicted = passed_back(once(evicted, *far_rows))
     both = [parked_piece(hops, 0, p1 + p2) for hops in near]
     z2 = [parked_piece(hops, p1, p2) for hops in far]
     early, third = kept_part(lengths, evicted, kept_rows, grad_out, 0, p1 + p2)

time: 90.7 us -> 107 us (1.18)
  waiting for transfers between devices: 40.2 us -> 55 us
    ppermute x6, waiting for transfers between devices: 19.9 us -> 47 us  [passed_back(): return lax.ppermute(rows, 'section', pairs)]
    ppermute x6, waiting for transfers between devices: 20.3 us -> 8.04 us  [shifted(): return lax.ppermute(rows, ('section', 'tp'), pairs)]
    ppermute x6, starting transfers between devices: 5.7 us -> 3.93 us  [passed_back(): return lax.ppermute(rows, 'section', pairs)]
    ppermute x6, starting transfers between devices: 11.6 us -> 13.2 us  [shifted(): return lax.ppermute(rows, ('section', 'tp'), pairs)]
  transfers between devices with their start and end apart: 13 -> 13, of which waited for: 9 -> 6; matrix products, arithmetic and copies ran while one was open for 4% -> 1% of each run, Pallas kernels for 24% -> 20%
where the time goes in v5:
time: 107 us; the launch traced here: 106 us
  waiting for transfers between devices  55 us (51%)
  Pallas kernels  24.4 us (23%)
  starting transfers between devices  21.9 us (20%)
  local copies, waits for them, and re-layouts  3.57 us (3%)
    ppermute x6, waiting for transfers between devices, passed_back(): return lax.ppermute(rows, 'section', pairs)  47 us
    ppermute x6, starting transfers between devices, shifted(): return lax.ppermute(rows, ('section', 'tp'), pairs)  13.2 us
    pallas_call x2, Pallas kernels, parked_part(): pl.pallas_call(functools.partial(parked_kernel, (far_at, far_at, at, at))...  8.39 us
    pallas_call x1, Pallas kernels, kept_part(): pl.pallas_call(kept_kernel, grid_spec=pltpu.PrefetchScalarGridSpec(num_sc...  8.21 us
    ppermute x6, waiting for transfers between devices, shifted(): return lax.ppermute(rows, ('section', 'tp'), pairs)  8.04 us
    pallas_call x3, Pallas kernels, place(): pl.pallas_call(functools.partial(place_kernel, slots, firsts, flagged), i...  7.85 us
    ppermute x1, starting transfers between devices, across_ends(): lax.ppermute(rows, 'section', [(half - 1, sections - 1), (sections - 1, h...  4.75 us
    ppermute x6, starting transfers between devices, passed_back(): return lax.ppermute(rows, 'section', pairs)  3.93 us
  transfers between devices with their start and end apart: 13, of which 6 were waited for; matrix products, arithmetic and copies ran while one was open for 1% of the time, Pallas kernels for 20%

profile of v5, /device:TPU:63, one launch (start us, length us, event | category | flops | bytes accessed | tf_op | source)
XLA Modules:
  0.0 106.0 jit_solution(9995260478791895679)
XLA Ops:
  0.0 2.5 %constant_dynamic-slice_fusion = (bf16[64,2304]{1,0:T(8,128)(2,1)}, bf16[64,2304]{1,0:T(8,128)(2,1)}, bf16[64,2304]{1,0:T(8,128)(2,1)}, bf16[64,2304]{1,0:T(8,128)(2,1)}) fusion(bf16[64,18432]{1,0:T(8,128)(2,1)} %param.6, s32[]{:T(128)S(6)} %select_n.51, s32[]{:T(128)S(6)} %select_n.45, s32[]{:T(128)S(6)} %select_n.43, s32[]{:T(128)S(6)} %select_n.50), kind=kLoop, calls=%fused_computation | loop fusion | bytes 2359312 | tf_op jit(solution)/shard_map/dynamic_slice | solution.py:292
  2.5 5.6 %collective-permute-start.2 = (bf16[64,2304]{1,0:T(8,128)(2,1)}, bf16[64,2304]{1,0:T(8,128)(2,1)}, u32[]{:S(2)}, u32[]{:S(2)}) collective-permute-start(bf16[64,2304]{1,0:T(8,128)(2,1)} %get-tuple-element.27), channel_id=1, source_target_pairs={{0,129},{1,130},{2,131},{3,128},{4,133},{5,134},{6,135},{7,132},{8... | collective-permute-start | bytes 884744 | tf_op jit(solution)/shard_map/ppermute | solution.py:279
  8.0 1.0 collective-permute-start
  9.0 1.1 %constant_dynamic-slice_fusion.2 = (bf16[64,4608]{1,0:T(8,128)(2,1)}, bf16[64,4608]{1,0:T(8,128)(2,1)}) fusion(bf16[64,18432]{1,0:T(8,128)(2,1)S(1)} %copy-done.1, s32[]{:T(128)S(6)} %select_n.49, s32[]{:T(128)S(6)} %select_n.48), kind=kLoop, calls=%fused_computation.2 | loop fusion | bytes 2359304 | tf_op jit(solution)/shard_map/dynamic_slice | solution.py:292
  10.1 0.8 collective-permute-start.4
  10.9 0.6 collective-permute-start.5
  12.2 8.2 %kept_grads.1 = (bf16[256,4608]{1,0:T(8,128)(2,1)S(1)}, bf16[128,4608]{1,0:T(8,128)(2,1)}) custom-call(s32[3]{0:T(128)S(1)} %copy-done, s32[1]{0:T(128)S(6)} %copy.10.evicted, bf16[384,4608]{1,0:T(8,128)(2,1)} %rows.1, bf16[512,1536]{1,0:T(8,128)(2,1)} %g1.5, bf16[512,1536]{1,0:T(8,128)(2,1)} %g1.5, bf16[512,1536]{1,0:T(8,128)(2,1)} %g1.5), custom_call_target="tpu_custom_call" | custom-call | flops 12000000000 | bytes 1048576 | tf_op jit(solution)/shard_map/kept_grads/pallas_call | solution.py:150
  20.4 6.7 %collective-permute-done.evicted = s32[1]{0:T(128)} collective-permute-done((s32[1]{0:T(128)}, s32[1]{0:T(128)}, u32[]{:S(2)}, u32[]{:S(2)}) %collective-permute-start) | collective-permute-done | bytes 36 | tf_op jit(solution)/shard_map/ppermute | solution.py:283
  27.2 6.2 %collective-permute-start.7 = (bf16[64,2304]{1,0:T(8,128)(2,1)}, bf16[64,2304]{1,0:T(8,128)(2,1)S(1)}, u32[]{:S(2)}, u32[]{:S(2)}) collective-permute-start(bf16[64,2304]{1,0:T(8,128)(2,1)} %get-tuple-element.28), channel_id=1, source_target_pairs={{0,129},{1,130},{2,131},{3,128},{4,133},{5,134},{6,135},{7,132},{8... | collective-permute-start | bytes 884744 | tf_op jit(solution)/shard_map/ppermute | solution.py:279
  33.4 5.5 %collective-permute-done.4.r2 = bf16[64,4608]{1,0:T(8,128)(2,1)S(1)} collective-permute-done((bf16[64,4608]{1,0:T(8,128)(2,1)}, bf16[64,4608]{1,0:T(8,128)(2,1)S(1)}, u32[]{:S(2)}, u32[]{:S(2)}) %collective-permute-start.4) | collective-permute-done | bytes 589856 | tf_op jit(solution)/shard_map/ppermute | solution.py:279
  38.9 2.6 %collective-permute-done.5.r3 = bf16[64,4608]{1,0:T(8,128)(2,1)S(1)} collective-permute-done((bf16[64,4608]{1,0:T(8,128)(2,1)}, bf16[64,4608]{1,0:T(8,128)(2,1)S(1)}, u32[]{:S(2)}, u32[]{:S(2)}) %collective-permute-start.5) | collective-permute-done | bytes 589856 | tf_op jit(solution)/shard_map/ppermute | solution.py:279
  41.4 4.2 %parked_grads.2 = (bf16[128,2304]{1,0:T(8,128)(2,1)S(1)}, bf16[128,2304]{1,0:T(8,128)(2,1)S(1)}) custom-call(s32[3]{0:T(128)S(1)} %copy-done, s32[1]{0:T(128)S(6)} %copy.10.evicted, s32[4]{0:T(128)S(1)} %pad_add_fusion.quarters, bf16[64,2304]{1,0:T(8,128)(2,1)} %collective-permute-done.2.r0, bf16[64,2304]{1,0:T(8,128)(2,1)} %collective-permute-done.3.r1, ...), custom_call_target="tpu_custom_call" | custom-call | flops 24000000000 | bytes 1048576 | tf_op jit(solution)/shard_map/parked_grads/pallas_call | solution.py:199
  45.7 2.7 %collective-permute-start.11 = (bf16[128,2304]{1,0:T(8,128)(2,1)S(1)}, bf16[128,2304]{1,0:T(8,128)(2,1)S(1)}, u32[]{:S(2)}, u32[]{:S(2)}) collective-permute-start(bf16[128,2304]{1,0:T(8,128)(2,1)S(1)} %get-tuple-element.19), channel_id=1, source_target_pairs={{0,252},{4,0},{8,4},{12,8},{16,12},{20,16},{24,20},{28,24},{32,28}... | collective-permute-start | bytes 1769480 | tf_op jit(solution)/shard_map/ppermute | solution.py:283
  48.4 0.1 collective-permute-start.12
  48.5 22.8 %collective-permute-done.1.refs_0_ = bf16[256,4608]{1,0:T(8,128)(2,1)S(1)} collective-permute-done((bf16[256,4608]{1,0:T(8,128)(2,1)S(1)}, bf16[256,4608]{1,0:T(8,128)(2,1)S(1)}, u32[]{:S(2)}, u32[]{:S(2)}) %collective-permute-start.1) | collective-permute-done | bytes 2359328 | tf_op jit(solution)/shard_map/ppermute | solution.py:283
  71.3 4.8 %collective-permute-start.6 = (bf16[256,4608]{1,0:T(8,128)(2,1)S(1)}, bf16[256,4608]{1,0:T(8,128)(2,1)S(1)}, u32[]{:S(2)}, u32[]{:S(2)}) collective-permute-start(bf16[256,4608]{1,0:T(8,128)(2,1)S(1)} %collective-permute-done.1.refs_0_), channel_id=1, source_target_pairs={{124,252},{252,124},{125,253},{253,125},{126,254},{254,126},{127,2... | collective-permute-start | bytes 7077896 | tf_op jit(solution)/shard_map/ppermute | solution.py:286
  76.1 2.6 %place_rows.3.refs_2_ = bf16[512,4608]{1,0:T(8,128)(2,1)} custom-call(s32[3]{0:T(128)S(1)} %copy-done, s32[1]{0:T(128)} %collective-permute-done.evicted, s32[1]{0:T(128)} %bitcast.flag, bf16[256,4608]{1,0:T(8,128)(2,1)S(1)} %collective-permute-done.1.refs_0_), custom_call_target="tpu_custom_call" | custom-call | flops 1000000000 | bytes 1048576 | tf_op jit(solution)/shard_map/place_rows/pallas_call | solution.py:252
  78.7 4.2 %parked_grads.3 = (bf16[128,2304]{1,0:T(8,128)(2,1)S(1)}, bf16[128,2304]{1,0:T(8,128)(2,1)S(1)}) custom-call(s32[3]{0:T(128)S(1)} %copy-done, s32[1]{0:T(128)S(6)} %copy.10.evicted, s32[4]{0:T(128)S(1)} %pad_add_fusion.quarters, bf16[64,2304]{1,0:T(8,128)(2,1)S(1)} %collective-permute-done.7.r0, bf16[64,2304]{1,0:T(8,128)(2,1)S(1)} %collective-permute-done.8.r1, ...), custom_call_target="tpu_custom_call" | custom-call | flops 48000000000 | bytes 1048576 | tf_op jit(solution)/shard_map/parked_grads/pallas_call | solution.py:199
  82.9 0.1 collective-permute-start.9
  83.0 0.1 collective-permute-start.10
  83.1 2.2 %place_rows.4.refs_3_ = bf16[512,4608]{1,0:T(8,128)(2,1)} custom-call(s32[3]{0:T(128)S(1)} %copy-done, s32[1]{0:T(128)} %collective-permute-done.evicted, s32[1]{0:T(128)} %bitcast.flag, bf16[128,2304]{1,0:T(8,128)(2,1)S(1)} %collective-permute-done.11.refs_0_, ...), custom_call_target="tpu_custom_call", output_to_operand_aliasing={{}: (5, {})} | custom-call | flops 1000000000 | bytes 1048576 | tf_op jit(solution)/shard_map/place_rows/pallas_call | solution.py:252
  85.3 11.2 %collective-permute-done.9.refs_1_ = bf16[128,2304]{1,0:T(8,128)(2,1)S(1)} collective-permute-done((bf16[128,2304]{1,0:T(8,128)(2,1)S(1)}, bf16[128,2304]{1,0:T(8,128)(2,1)S(1)}, u32[]{:S(2)}, u32[]{:S(2)}) %collective-permute-start.9) | collective-permute-done | bytes 589856 | tf_op jit(solution)/shard_map/ppermute | solution.py:283
  96.5 6.3 %collective-permute-done.10.refs_2_ = bf16[128,2304]{1,0:T(8,128)(2,1)S(1)} collective-permute-done((bf16[128,2304]{1,0:T(8,128)(2,1)S(1)}, bf16[128,2304]{1,0:T(8,128)(2,1)S(1)}, u32[]{:S(2)}, u32[]{:S(2)}) %collective-permute-start.10) | collective-permute-done | bytes 589856 | tf_op jit(solution)/shard_map/ppermute | solution.py:283
  102.8 3.0 %place_rows.5 = bf16[512,4608]{1,0:T(8,128)(2,1)} custom-call(s32[3]{0:T(128)S(1)} %copy-done, s32[1]{0:T(128)} %collective-permute-done.evicted, s32[1]{0:T(128)} %bitcast.flag, bf16[256,4608]{1,0:T(8,128)(2,1)S(1)} %collective-permute-done.6.refs_0_, bf16[128,2304]{1,0:T(8,128)(2,1)S(1)} %collective-permute-done.9.refs_1_, ...), custom_call_target="tpu_custom_call", output_to_operand_aliasing={{}: (6, {})} | custom-call | flops 1000000000 | bytes 1048576 | tf_op jit(solution)/shard_map/place_rows/pallas_call | solution.py:252
  (15 shorter events, 0.1 us)
Async XLA Ops:
  0.0 9.0 %copy-start.1 = (bf16[64,18432]{1,0:T(8,128)(2,1)S(1)}, bf16[64,18432]{1,0:T(8,128)(2,1)}, u32[]{:S(2)}) copy-start(bf16[64,18432]{1,0:T(8,128)(2,1)} %param.6) | copy-start | bytes 7077892
  0.0 12.2 %copy-start = (s32[3]{0:T(128)S(1)}, s32[3]{0:T(128)}, u32[]{:S(2)}) copy-start(s32[3]{0:T(128)} %lengths.10) | copy-start | bytes 40
  2.5 24.7 %collective-permute-start.2 = (bf16[64,2304]{1,0:T(8,128)(2,1)}, bf16[64,2304]{1,0:T(8,128)(2,1)}, u32[]{:S(2)}, u32[]{:S(2)}) collective-permute-start(bf16[64,2304]{1,0:T(8,128)(2,1)} %get-tuple-element.27), channel_id=1, source_target_pairs={{0,129},{1,130},{2,131},{3,128},{4,133},{5,134},{6,135},{7,132},{8... | collective-permute-start | bytes 884744 | tf_op jit(solution)/shard_map/ppermute | solution.py:279
  8.0 25.4 %collective-permute-start.3 = (bf16[64,2304]{1,0:T(8,128)(2,1)}, bf16[64,2304]{1,0:T(8,128)(2,1)}, u32[]{:S(2)}, u32[]{:S(2)}) collective-permute-start(bf16[64,2304]{1,0:T(8,128)(2,1)} %get-tuple-element.26), channel_id=1, source_target_pairs={{0,130},{1,131},{2,128},{3,129},{4,134},{5,135},{6,132},{7,133},{8... | collective-permute-start | bytes 884744 | tf_op jit(solution)/shard_map/ppermute | solution.py:279
  8.0 19.1 %collective-permute-start = (s32[1]{0:T(128)}, s32[1]{0:T(128)}, u32[]{:S(2)}, u32[]{:S(2)}) collective-permute-start(s32[1]{0:T(128)} %param.9), channel_id=1, source_target_pairs={{0,252},{4,0},{8,4},{12,8},{16,12},{20,16},{24,20},{28,24},{32,28}... | collective-permute-start | bytes 20 | tf_op jit(solution)/shard_map/ppermute | solution.py:283
  10.1 28.8 %collective-permute-start.4 = (bf16[64,4608]{1,0:T(8,128)(2,1)}, bf16[64,4608]{1,0:T(8,128)(2,1)S(1)}, u32[]{:S(2)}, u32[]{:S(2)}) collective-permute-start(bf16[64,4608]{1,0:T(8,128)(2,1)} %get-tuple-element.30), channel_id=1, source_target_pairs={{0,128},{1,129},{2,130},{3,131},{4,132},{5,133},{6,134},{7,135},{8... | collective-permute-start | bytes 1769480 | tf_op jit(solution)/shard_map/ppermute | solution.py:279
  10.9 30.5 %collective-permute-start.5 = (bf16[64,4608]{1,0:T(8,128)(2,1)}, bf16[64,4608]{1,0:T(8,128)(2,1)S(1)}, u32[]{:S(2)}, u32[]{:S(2)}) collective-permute-start(bf16[64,4608]{1,0:T(8,128)(2,1)} %get-tuple-element.29), channel_id=1, source_target_pairs={{0,131},{1,128},{2,129},{3,130},{4,135},{5,132},{6,133},{7,134},{8... | collective-permute-start | bytes 1769480 | tf_op jit(solution)/shard_map/ppermute | solution.py:279
  27.1 44.2 %collective-permute-start.1 = (bf16[256,4608]{1,0:T(8,128)(2,1)S(1)}, bf16[256,4608]{1,0:T(8,128)(2,1)S(1)}, u32[]{:S(2)}, u32[]{:S(2)}) collective-permute-start(bf16[256,4608]{1,0:T(8,128)(2,1)S(1)} %get-tuple-element.17), channel_id=1, source_target_pairs={{0,124},{4,0},{8,4},{12,8},{16,12},{20,16},{24,20},{28,24},{32,28}... | collective-permute-start | bytes 7077896 | tf_op jit(solution)/shard_map/ppermute | solution.py:283
  27.2 51.5 %collective-permute-start.7 = (bf16[64,2304]{1,0:T(8,128)(2,1)}, bf16[64,2304]{1,0:T(8,128)(2,1)S(1)}, u32[]{:S(2)}, u32[]{:S(2)}) collective-permute-start(bf16[64,2304]{1,0:T(8,128)(2,1)} %get-tuple-element.28), channel_id=1, source_target_pairs={{0,129},{1,130},{2,131},{3,128},{4,133},{5,134},{6,135},{7,132},{8... | collective-permute-start | bytes 884744 | tf_op jit(solution)/shard_map/ppermute | solution.py:279
  33.4 45.3 %collective-permute-start.8 = (bf16[64,2304]{1,0:T(8,128)(2,1)}, bf16[64,2304]{1,0:T(8,128)(2,1)S(1)}, u32[]{:S(2)}, u32[]{:S(2)}) collective-permute-start(bf16[64,2304]{1,0:T(8,128)(2,1)} %get-tuple-element.25), channel_id=1, source_target_pairs={{0,130},{1,131},{2,128},{3,129},{4,134},{5,135},{6,132},{7,133},{8... | collective-permute-start | bytes 884744 | tf_op jit(solution)/shard_map/ppermute | solution.py:279
  45.7 37.4 %collective-permute-start.11 = (bf16[128,2304]{1,0:T(8,128)(2,1)S(1)}, bf16[128,2304]{1,0:T(8,128)(2,1)S(1)}, u32[]{:S(2)}, u32[]{:S(2)}) collective-permute-start(bf16[128,2304]{1,0:T(8,128)(2,1)S(1)} %get-tuple-element.19), channel_id=1, source_target_pairs={{0,252},{4,0},{8,4},{12,8},{16,12},{20,16},{24,20},{28,24},{32,28}... | collective-permute-start | bytes 1769480 | tf_op jit(solution)/shard_map/ppermute | solution.py:283
  48.4 34.7 %collective-permute-start.12 = (bf16[128,2304]{1,0:T(8,128)(2,1)S(1)}, bf16[128,2304]{1,0:T(8,128)(2,1)S(1)}, u32[]{:S(2)}, u32[]{:S(2)}) collective-permute-start(bf16[128,2304]{1,0:T(8,128)(2,1)S(1)} %get-tuple-element.20), channel_id=1, source_target_pairs={{0,252},{4,0},{8,4},{12,8},{16,12},{20,16},{24,20},{28,24},{32,28}... | collective-permute-start | bytes 1769480 | tf_op jit(solution)/shard_map/ppermute | solution.py:283
  71.3 31.5 %collective-permute-start.6 = (bf16[256,4608]{1,0:T(8,128)(2,1)S(1)}, bf16[256,4608]{1,0:T(8,128)(2,1)S(1)}, u32[]{:S(2)}, u32[]{:S(2)}) collective-permute-start(bf16[256,4608]{1,0:T(8,128)(2,1)S(1)} %collective-permute-done.1.refs_0_), channel_id=1, source_target_pairs={{124,252},{252,124},{125,253},{253,125},{126,254},{254,126},{127,2... | collective-permute-start | bytes 7077896 | tf_op jit(solution)/shard_map/ppermute | solution.py:286
  82.9 13.6 %collective-permute-start.9 = (bf16[128,2304]{1,0:T(8,128)(2,1)S(1)}, bf16[128,2304]{1,0:T(8,128)(2,1)S(1)}, u32[]{:S(2)}, u32[]{:S(2)}) collective-permute-start(bf16[128,2304]{1,0:T(8,128)(2,1)S(1)} %get-tuple-element.23), channel_id=1, source_target_pairs={{0,252},{4,0},{8,4},{12,8},{16,12},{20,16},{24,20},{28,24},{32,28}... | collective-permute-start | bytes 1769480 | tf_op jit(solution)/shard_map/ppermute | solution.py:283
  83.0 19.8 %collective-permute-start.10 = (bf16[128,2304]{1,0:T(8,128)(2,1)S(1)}, bf16[128,2304]{1,0:T(8,128)(2,1)S(1)}, u32[]{:S(2)}, u32[]{:S(2)}) collective-permute-start(bf16[128,2304]{1,0:T(8,128)(2,1)S(1)} %get-tuple-element.24), channel_id=1, source_target_pairs={{0,252},{4,0},{8,4},{12,8},{16,12},{20,16},{24,20},{28,24},{32,28}... | collective-permute-start | bytes 1769480 | tf_op jit(solution)/shard_map/ppermute | solution.py:283
